TPU v7x, 32 devices: a whole 2x2x4 slice. The times are simulated.
32 devices in a mesh: modes: 4 (over y, core), sites: 8 (over z, x).
Axes of the slice: x: 2, y: 2, z: 4, core: 2. Of those that a mesh axis runs over, the one named last changes fastest.
Arguments:
- wave_state: float32 [4, 32, 32768], P(None, 'modes', 'sites'), may hold values from -6 to 6
- potential: float32 [32768], P('sites'), may hold values from -0.5 to 0.5
- spin_angle: float32 [32768], P('sites'), may hold values from -3.140625 to 3.140625
- magnet: float32 [3, 32768], P(None, 'sites'), may hold values from -0.6 to 0.6
- magnetic_mask: int32 [32768], P('sites'), may hold values 0 or 1
- mode_weight: float32 [32], P('modes'), may hold values from 0.5 to 2
- source_amp: float32 [4, 32], P(None, 'modes'), may hold values from -6 to 6
- mode_group: int32 [32], P('modes'), may hold values from 0 to 7
- energies: float32 [8], replicated, may hold values from -2 to 2
- lead_site: int32 [32], P('modes'), may hold values from 0 to 32767
Outputs:
- next_state: float32 [4, 32, 32768], P(None, 'modes', 'sites')
- densities: float32 [5, 32768], P(None, 'sites')
- magnet_next: float32 [3, 32768], P(None, 'sites')
All inputs are finite; a program needn't handle non-finite values. No bound on the sum of `magnetic_mask` on one device may be relied on, other than what follows from the above.
Results may differ from a plain program's by a relative error of at most 0.0001.
Values sent between devices are 32-bit elements; how exact they have to be, the bound alone decides.
No kernel may reach another device: no remote copies, remote signals or barrier semaphores. Data moves between devices by JAX's collectives and lax.ppermute only.
A program may use at most 64 MiB of HBM per device.

v0:
```python
import math

import jax
import jax.numpy as jnp
from jax import lax
from jax.sharding import PartitionSpec as P

time_step = 0.6
start_time = 10.0
exchange_coupling = 0.5


def extended(cells, sides, width):
    for axis, dim in sides:
        count = lax.axis_size(axis)
        ends = count - 1
        head = lax.slice_in_dim(cells, 0, width, axis=dim)
        tail = lax.slice_in_dim(cells, cells.shape[dim] - width, cells.shape[dim], axis=dim)
        cells = jnp.concatenate(
            [
                lax.ppermute(tail, axis, [(i, (i + 1) % count) for i in range(ends)]),
                cells,
                lax.ppermute(head, axis, [((i + 1) % count, i) for i in range(ends)]),
            ],
            axis=dim,
        )
    return cells


def rotate_back(spinor, cosine, sine_term):
    shaped = spinor.reshape((2, 2) + spinor.shape[1:])
    spin_up = shaped[:, 0]
    spin_down = shaped[:, 1]
    turned = jnp.stack(
        [cosine * spin_up + sine_term * spin_down, cosine * spin_down - sine_term * spin_up], axis=1
    )
    return turned.reshape(spinor.shape)


def rotate_fore(spinor, cosine, sine_term):
    shaped = spinor.reshape((2, 2) + spinor.shape[1:])
    spin_up = shaped[:, 0]
    spin_down = shaped[:, 1]
    turned = jnp.stack(
        [cosine * spin_up - sine_term * spin_down, sine_term * spin_up + cosine * spin_down], axis=1
    )
    return turned.reshape(spinor.shape)


def exchange_term(spinor, sd_field):
    up_real, down_real, up_imag, down_imag = (spinor[0], spinor[1], spinor[2], spinor[3])
    field_x, field_y, field_z = (sd_field[0], sd_field[1], sd_field[2])
    out_up_real = field_z * up_real + field_x * down_real + field_y * down_imag
    out_down_real = field_x * up_real - field_y * up_imag - field_z * down_real
    out_up_imag = field_z * up_imag + field_x * down_imag - field_y * down_real
    out_down_imag = field_x * up_imag + field_y * up_real - field_z * down_imag
    return jnp.stack([out_up_real, out_down_real, out_up_imag, out_down_imag])


def source_field(offset, amplitude, energy, region):
    phase_angle = energy * (start_time + offset)
    cosine_phase = jnp.cos(phase_angle)
    sine_phase = jnp.sin(phase_angle)
    amp_real = amplitude[0:2]
    amp_imag = amplitude[2:4]
    real_part = amp_real * cosine_phase + amp_imag * sine_phase
    imag_part = amp_imag * cosine_phase - amp_real * sine_phase
    joined = jnp.concatenate([real_part, imag_part], axis=0)
    return joined[:, :, None] * region[None]


def rate(spinor, left_w, right_w, cosine, sine_term, potential, sd_field, source):
    hamil_term = (
        potential * spinor
        + exchange_term(spinor, sd_field)
        - rotate_fore(left_w + right_w, cosine, sine_term)
        + source
    )
    return jnp.concatenate([hamil_term[2:], -hamil_term[:2]], axis=0)


def densities_of(spinor, right_w, cosine, sine_term, weight_vec):
    up_real, down_real, up_imag, down_imag = (spinor[0], spinor[1], spinor[2], spinor[3])
    hopped = rotate_fore(right_w, cosine, sine_term)
    charge = up_real * up_real + down_real * down_real + up_imag * up_imag + down_imag * down_imag
    spin_x = 2.0 * (up_real * down_real + up_imag * down_imag)
    spin_y = 2.0 * (up_real * down_imag - up_imag * down_real)
    spin_z = up_real * up_real + up_imag * up_imag - down_real * down_real - down_imag * down_imag
    current = 2.0 * (
        up_real * hopped[2] + down_real * hopped[3] - up_imag * hopped[0] - down_imag * hopped[1]
    )
    stacked = jnp.stack([charge, spin_x, spin_y, spin_z, current])
    return jnp.sum(stacked * weight_vec[None, :, None], axis=1)


def advance(magnet, mask_float, totals):
    field_h = exchange_coupling * totals[1:4]
    torque = jnp.stack(
        [
            magnet[1] * field_h[2] - magnet[2] * field_h[1],
            magnet[2] * field_h[0] - magnet[0] * field_h[2],
            magnet[0] * field_h[1] - magnet[1] * field_h[0],
        ]
    )
    return magnet - time_step * (mask_float * torque)


def source_region(positions, lead_site, region_span):
    return (
        (positions[None, :] >= lead_site[:, None])
        & (positions[None, :] < lead_site[:, None] + region_span)
    ).astype(jnp.float32)


def local(
    wave_state,
    potential,
    spin_angle,
    magnet,
    magnetic_mask,
    mode_weight,
    source_amp,
    mode_group,
    energies,
    lead_site,
):
    local_sites = wave_state.shape[2]
    local_modes = wave_state.shape[1]
    site_count = lax.axis_size("sites")
    mode_count = lax.axis_size("modes")
    first_site = lax.axis_index("sites") * local_sites
    wire_sites = local_sites * site_count
    region_span = wire_sites // 8
    all_modes = local_modes * mode_count
    mask_float = magnetic_mask.astype(jnp.float32)
    group_ids = jnp.arange(energies.shape[0], dtype=jnp.int32)
    mode_energy = jnp.sum(
        jnp.where(
            mode_group[:, None] == group_ids[None, :],
            energies[None, :],
            jnp.zeros_like(energies)[None, :],
        ),
        axis=1,
    )
    cosine = jnp.cos(spin_angle)
    sine_term = jnp.sin(spin_angle)
    positions = first_site + jnp.arange(local_sites, dtype=jnp.int32)
    region = source_region(positions, lead_site, region_span)
    sd_field = exchange_coupling * mask_float * magnet

    def slope(spin_state, offset):
        weighted = rotate_back(spin_state, cosine, sine_term)
        padded = extended(weighted, (("sites", 2),), 1)
        source = source_field(offset, source_amp, mode_energy, region)
        return (
            rate(
                spin_state,
                padded[..., :-2],
                padded[..., 2:],
                cosine,
                sine_term,
                potential,
                sd_field,
                source,
            ),
            padded,
        )

    slope_one, padded_one = slope(wave_state, 0.0)
    slope_two, ignored = slope(wave_state + 0.5 * time_step * slope_one, 0.5 * time_step)
    slope_three, ignored = slope(wave_state + 0.5 * time_step * slope_two, 0.5 * time_step)
    slope_four, ignored = slope(wave_state + time_step * slope_three, time_step)
    next_state = wave_state + time_step / 6.0 * (
        slope_one + 2.0 * slope_two + 2.0 * slope_three + slope_four
    )
    right_w = padded_one[..., 2:]
    root_scale = 1.0 / math.sqrt(all_modes)
    row_scale = jnp.array(
        [1.0 / all_modes, root_scale, root_scale, root_scale, root_scale], jnp.float32
    )
    partial_value = (
        densities_of(wave_state, right_w, cosine, sine_term, mode_weight) * row_scale[:, None]
    )
    totals = lax.psum(partial_value, "modes")
    magnet_next = advance(magnet, mask_float, totals)
    return (next_state, totals, magnet_next)


def solution(mesh):
    return jax.shard_map(
        local,
        mesh=mesh,
        in_specs=(
            P(None, "modes", "sites"),
            P("sites"),
            P("sites"),
            P(None, "sites"),
            P("sites"),
            P("modes"),
            P(None, "modes"),
            P("modes"),
            P(),
            P("modes"),
        ),
        out_specs=(P(None, "modes", "sites"), P(None, "sites"), P(None, "sites")),
        check_vma=False,
    )
```

profile of v0, /device:TPU:0, one launch (start us, length us, event | category | flops | bytes accessed | tf_op | source)
XLA Modules:
  0.0 74.5 jit_solution(13564782049816135281)
XLA Ops:
  7.2 0.8 %fusion.28 = (f32[4096]{0:T(1024)S(1)}, f32[4096]{0:T(1024)S(1)}) fusion(f32[4096]{0:T(1024)} %param.13), kind=kLoop, calls=%fused_computation.133 | loop fusion | bytes 49152 | tf_op jit(solution)/shard_map/cos | solution.py:145
  8.0 1.1 %multiply_add_fusion.13 = (f32[2,1,8,4096]{3,2,1,0:T(8,128)S(1)}, f32[2,1,8,4096]{3,2,1,0:T(8,128)S(1)}) fusion(f32[2,2,8,4096]{3,2,1,0:T(8,128)} %bitcast.25, f32[4096]{0:T(1024)S(1)} %get-tuple-element.65, f32[4096]{0:T(1024)S(1)} %get-tuple-element.64), kind=kLoop, calls=%fused_computation.64 | loop fusion | flops 393216 | bytes 1081344 | tf_op jit(solution)/shard_map/add | solution.py:35
  9.2 5.0 %collective-permute-start = (f32[4,8,1]{2,1,0:T(8,128)S(1)}, f32[4,8,1]{2,1,0:T(8,128)S(1)}, u32[]{:S(2)}, u32[]{:S(2)}) collective-permute-start(f32[4,8,1]{2,1,0:T(8,128)S(1)} %get-tuple-element.55), channel_id=1, source_target_pairs={{0,1},{1,2},{2,3},{3,4},{4,5},{5,6},{6,7},{8,9},{9,10},{10,11},{11... | collective-permute-start | bytes 392 | tf_op jit(solution)/shard_map/ppermute | solution.py:21
  14.2 1.3 %collective-permute-start.1 = (f32[4,8,1]{2,1,0:T(8,128)S(1)}, f32[4,8,1]{2,1,0:T(8,128)S(1)}, u32[]{:S(2)}, u32[]{:S(2)}) collective-permute-start(f32[4,8,1]{2,1,0:T(8,128)S(1)} %get-tuple-element.54), channel_id=1, source_target_pairs={{1,0},{2,1},{3,2},{4,3},{5,4},{6,5},{7,6},{9,8},{10,9},{11,10},{12... | collective-permute-start | bytes 392 | tf_op jit(solution)/shard_map/ppermute | solution.py:23
  15.9 0.6 copy-done.13
  16.8 0.6 copy-done.10
  17.5 0.7 copy-done.9
  18.2 0.6 pad_maximum_fusion.20
  18.8 0.6 pad_maximum_fusion.22
  19.4 0.6 convert_element_type.10
  20.6 0.6 copy-done.3
  21.7 0.7 fusion.24
  22.3 5.1 %collective-permute-start.2 = (f32[4,8,1]{2,1,0:T(8,128)}, f32[4,8,1]{2,1,0:T(8,128)}, u32[]{:S(2)}, u32[]{:S(2)}) collective-permute-start(f32[4,8,1]{2,1,0:T(8,128)} %get-tuple-element.50), channel_id=1, source_target_pairs={{0,1},{1,2},{2,3},{3,4},{4,5},{5,6},{6,7},{8,9},{9,10},{10,11},{11... | collective-permute-start | bytes 392 | tf_op jit(solution)/shard_map/ppermute | solution.py:21
  27.5 1.3 %collective-permute-start.3 = (f32[4,8,1]{2,1,0:T(8,128)}, f32[4,8,1]{2,1,0:T(8,128)}, u32[]{:S(2)}, u32[]{:S(2)}) collective-permute-start(f32[4,8,1]{2,1,0:T(8,128)} %get-tuple-element.51), channel_id=1, source_target_pairs={{1,0},{2,1},{3,2},{4,3},{5,4},{6,5},{7,6},{9,8},{10,9},{11,10},{12... | collective-permute-start | bytes 392 | tf_op jit(solution)/shard_map/ppermute | solution.py:23
  28.8 0.6 copy-done.12
  29.7 0.4 copy-done.11
  30.1 0.7 broadcast_multiply_fusion
  30.8 2.6 %collective-permute-done.3 = f32[4,8,1]{2,1,0:T(8,128)} collective-permute-done((f32[4,8,1]{2,1,0:T(8,128)}, f32[4,8,1]{2,1,0:T(8,128)}, u32[]{:S(2)}, u32[]{:S(2)}) %collective-permute-start.3) | collective-permute-done | bytes 160 | tf_op jit(solution)/shard_map/ppermute | solution.py:23
  33.4 1.1 %fusion.2 = f32[4,8,4096]{2,1,0:T(8,128)S(1)} fusion(f32[4,8,1]{2,1,0:T(8,128)} %collective-permute-done.3, f32[4,8,4096]{2,1,0:T(8,128)S(1)} %bitcast.32, f32[4,8,1]{2,1,0:T(8,128)} %collective-permute-done.2), kind=kLoop, calls=%fused_computation.10 | loop fusion | flops 393216 | bytes 1048832 | tf_op jit(solution)/shard_map/add | solution.py:76
  34.6 0.7 copy-done.4
  35.7 4.7 %collective-permute-start.4 = (f32[4,8,1]{2,1,0:T(8,128)S(1)}, f32[4,8,1]{2,1,0:T(8,128)S(1)}, u32[]{:S(2)}, u32[]{:S(2)}) collective-permute-start(f32[4,8,1]{2,1,0:T(8,128)S(1)} %get-tuple-element.46), channel_id=1, source_target_pairs={{0,1},{1,2},{2,3},{3,4},{4,5},{5,6},{6,7},{8,9},{9,10},{10,11},{11... | collective-permute-start | bytes 392 | tf_op jit(solution)/shard_map/ppermute | solution.py:21
  40.4 1.3 %collective-permute-start.5 = (f32[4,8,1]{2,1,0:T(8,128)S(1)}, f32[4,8,1]{2,1,0:T(8,128)S(1)}, u32[]{:S(2)}, u32[]{:S(2)}) collective-permute-start(f32[4,8,1]{2,1,0:T(8,128)S(1)} %get-tuple-element.47), channel_id=1, source_target_pairs={{1,0},{2,1},{3,2},{4,3},{5,4},{6,5},{7,6},{9,8},{10,9},{11,10},{12... | collective-permute-start | bytes 392 | tf_op jit(solution)/shard_map/ppermute | solution.py:23
  41.8 4.2 %collective-permute-done.5 = f32[4,8,1]{2,1,0:T(8,128)S(1)} collective-permute-done((f32[4,8,1]{2,1,0:T(8,128)S(1)}, f32[4,8,1]{2,1,0:T(8,128)S(1)}, u32[]{:S(2)}, u32[]{:S(2)}) %collective-permute-start.5) | collective-permute-done | bytes 160 | tf_op jit(solution)/shard_map/ppermute | solution.py:23
  47.0 2.9 %collective-permute-start.6 = (f32[4,8,1]{2,1,0:T(8,128)S(1)}, f32[4,8,1]{2,1,0:T(8,128)S(1)}, u32[]{:S(2)}, u32[]{:S(2)}) collective-permute-start(f32[4,8,1]{2,1,0:T(8,128)S(1)} %get-tuple-element.42), channel_id=1, source_target_pairs={{0,1},{1,2},{2,3},{3,4},{4,5},{5,6},{6,7},{8,9},{9,10},{10,11},{11... | collective-permute-start | bytes 392 | tf_op jit(solution)/shard_map/ppermute | solution.py:21
  49.9 1.3 %collective-permute-start.7 = (f32[4,8,1]{2,1,0:T(8,128)S(1)}, f32[4,8,1]{2,1,0:T(8,128)S(1)}, u32[]{:S(2)}, u32[]{:S(2)}) collective-permute-start(f32[4,8,1]{2,1,0:T(8,128)S(1)} %get-tuple-element.43), channel_id=1, source_target_pairs={{1,0},{2,1},{3,2},{4,3},{5,4},{6,5},{7,6},{9,8},{10,9},{11,10},{12... | collective-permute-start | bytes 392 | tf_op jit(solution)/shard_map/ppermute | solution.py:23
  51.3 4.2 %collective-permute-done.7 = f32[4,8,1]{2,1,0:T(8,128)S(1)} collective-permute-done((f32[4,8,1]{2,1,0:T(8,128)S(1)}, f32[4,8,1]{2,1,0:T(8,128)S(1)}, u32[]{:S(2)}, u32[]{:S(2)}) %collective-permute-start.7) | collective-permute-done | bytes 160 | tf_op jit(solution)/shard_map/ppermute | solution.py:23
  56.0 0.7 copy-done.8
  56.8 1.0 %fusion.11 = f32[4,8,4096]{2,1,0:T(8,128)} fusion(f32[4,8,4096]{2,1,0:T(8,128)S(1)} %copy-done, f32[2,8,4096]{2,1,0:T(8,128)S(1)} %get-tuple-element.41, f32[2,8,4096]{2,1,0:T(8,128)S(1)} %get-tuple-element.40, f32[2,8,4096]{2,1,0:T(8,128)S(1)} %get-tuple-element.45, f32[2,8,4096]{2,1,0:T(8,128)S(1)} %get-tuple-element.44, ...), kind=kLoop, calls=%fused_computation.38 | loop fusion | flops 1441792 | bytes 3145728 | tf_op jit(solution)/shard_map/add | solution.py:173
  57.8 7.2 %all-reduce.2.cloned.1.call-done = f32[5,4096]{1,0:T(8,128)} async-done(((f32[5,4096]{1,0:T(8,128)}), f32[5,4096]{1,0:T(8,128)}) %all-reduce.2.cloned.1.call-update) | async-done | bytes 81936 | tf_op jit(solution)/shard_map/psum | solution.py:184
  65.1 0.9 %slice_multiply_fusion.4 = f32[3,4096]{1,0:T(4,128)S(1)} fusion(f32[5,4096]{1,0:T(8,128)} %all-reduce.2.cloned.1.call-done), kind=kLoop, calls=%fused_computation.95 | loop fusion | flops 12288 | bytes 98304 | tf_op jit(solution)/shard_map/mul | solution.py:97
  66.1 0.7 fusion.18
  67.0 0.7 copy.19
  (80 shorter events, 4.6 us)
Async XLA Ops:
  7.2 57.9 %all-reduce.2.cloned.1.call-start = ((), (), s32[]{:S(2)}) async-start(), calls=%async_computation | async-start | bytes 262144 | tf_op jit(solution)/shard_map/psum | solution.py:184
  9.1 6.4 %copy-start.6 = (s32[4096]{0:T(1024)S(1)}, s32[4096]{0:T(1024)}, u32[]{:S(2)}) copy-start(s32[4096]{0:T(1024)} %param.15) | copy-start | bytes 49156
  9.1 6.5 %copy-start = (f32[4,8,4096]{2,1,0:T(8,128)S(1)}, f32[4,8,4096]{2,1,0:T(8,128)}, u32[]{:S(2)}) copy-start(f32[4,8,4096]{2,1,0:T(8,128)} %param.11) | copy-start | bytes 1572868
  9.2 6.4 %copy-start.1 = (f32[3,4096]{1,0:T(4,128)S(1)}, f32[3,4096]{1,0:T(4,128)}, u32[]{:S(2)}) copy-start(f32[3,4096]{1,0:T(4,128)} %param.14) | copy-start | bytes 147460
  9.2 10.7 %collective-permute-start = (f32[4,8,1]{2,1,0:T(8,128)S(1)}, f32[4,8,1]{2,1,0:T(8,128)S(1)}, u32[]{:S(2)}, u32[]{:S(2)}) collective-permute-start(f32[4,8,1]{2,1,0:T(8,128)S(1)} %get-tuple-element.55), channel_id=1, source_target_pairs={{0,1},{1,2},{2,3},{3,4},{4,5},{5,6},{6,7},{8,9},{9,10},{10,11},{11... | collective-permute-start | bytes 392 | tf_op jit(solution)/shard_map/ppermute | solution.py:21
  14.2 5.8 %collective-permute-start.1 = (f32[4,8,1]{2,1,0:T(8,128)S(1)}, f32[4,8,1]{2,1,0:T(8,128)S(1)}, u32[]{:S(2)}, u32[]{:S(2)}) collective-permute-start(f32[4,8,1]{2,1,0:T(8,128)S(1)} %get-tuple-element.54), channel_id=1, source_target_pairs={{1,0},{2,1},{3,2},{4,3},{5,4},{6,5},{7,6},{9,8},{10,9},{11,10},{12... | collective-permute-start | bytes 392 | tf_op jit(solution)/shard_map/ppermute | solution.py:23
  15.8 0.7 copy-start.13
  15.9 0.7 copy-start.14
  16.8 0.7 copy-start.10
  17.5 0.7 copy-start.9
  20.5 0.7 copy-start.3
  22.3 8.5 %collective-permute-start.2 = (f32[4,8,1]{2,1,0:T(8,128)}, f32[4,8,1]{2,1,0:T(8,128)}, u32[]{:S(2)}, u32[]{:S(2)}) collective-permute-start(f32[4,8,1]{2,1,0:T(8,128)} %get-tuple-element.50), channel_id=1, source_target_pairs={{0,1},{1,2},{2,3},{3,4},{4,5},{5,6},{6,7},{8,9},{9,10},{10,11},{11... | collective-permute-start | bytes 392 | tf_op jit(solution)/shard_map/ppermute | solution.py:21
  27.5 5.9 %collective-permute-start.3 = (f32[4,8,1]{2,1,0:T(8,128)}, f32[4,8,1]{2,1,0:T(8,128)}, u32[]{:S(2)}, u32[]{:S(2)}) collective-permute-start(f32[4,8,1]{2,1,0:T(8,128)} %get-tuple-element.51), channel_id=1, source_target_pairs={{1,0},{2,1},{3,2},{4,3},{5,4},{6,5},{7,6},{9,8},{10,9},{11,10},{12... | collective-permute-start | bytes 392 | tf_op jit(solution)/shard_map/ppermute | solution.py:23
  28.8 0.7 copy-start.12
  29.4 0.7 copy-start.11
  34.6 0.7 copy-start.4
  34.6 0.7 copy-start.7
  35.7 6.1 %collective-permute-start.4 = (f32[4,8,1]{2,1,0:T(8,128)S(1)}, f32[4,8,1]{2,1,0:T(8,128)S(1)}, u32[]{:S(2)}, u32[]{:S(2)}) collective-permute-start(f32[4,8,1]{2,1,0:T(8,128)S(1)} %get-tuple-element.46), channel_id=1, source_target_pairs={{0,1},{1,2},{2,3},{3,4},{4,5},{5,6},{6,7},{8,9},{9,10},{10,11},{11... | collective-permute-start | bytes 392 | tf_op jit(solution)/shard_map/ppermute | solution.py:21
  40.4 5.6 %collective-permute-start.5 = (f32[4,8,1]{2,1,0:T(8,128)S(1)}, f32[4,8,1]{2,1,0:T(8,128)S(1)}, u32[]{:S(2)}, u32[]{:S(2)}) collective-permute-start(f32[4,8,1]{2,1,0:T(8,128)S(1)} %get-tuple-element.47), channel_id=1, source_target_pairs={{1,0},{2,1},{3,2},{4,3},{5,4},{6,5},{7,6},{9,8},{10,9},{11,10},{12... | collective-permute-start | bytes 392 | tf_op jit(solution)/shard_map/ppermute | solution.py:23
  47.0 4.4 %collective-permute-start.6 = (f32[4,8,1]{2,1,0:T(8,128)S(1)}, f32[4,8,1]{2,1,0:T(8,128)S(1)}, u32[]{:S(2)}, u32[]{:S(2)}) collective-permute-start(f32[4,8,1]{2,1,0:T(8,128)S(1)} %get-tuple-element.42), channel_id=1, source_target_pairs={{0,1},{1,2},{2,3},{3,4},{4,5},{5,6},{6,7},{8,9},{9,10},{10,11},{11... | collective-permute-start | bytes 392 | tf_op jit(solution)/shard_map/ppermute | solution.py:21
  49.9 5.6 %collective-permute-start.7 = (f32[4,8,1]{2,1,0:T(8,128)S(1)}, f32[4,8,1]{2,1,0:T(8,128)S(1)}, u32[]{:S(2)}, u32[]{:S(2)}) collective-permute-start(f32[4,8,1]{2,1,0:T(8,128)S(1)} %get-tuple-element.43), channel_id=1, source_target_pairs={{1,0},{2,1},{3,2},{4,3},{5,4},{6,5},{7,6},{9,8},{10,9},{11,10},{12... | collective-permute-start | bytes 392 | tf_op jit(solution)/shard_map/ppermute | solution.py:23
  56.0 0.7 copy-start.8
  56.8 9.3 %copy-start.5 = (f32[4096]{0:T(1024)S(1)}, f32[4096]{0:T(1024)}, u32[]{:S(2)}) copy-start(f32[4096]{0:T(1024)} %convert_element_type.10) | copy-start | bytes 49156
  66.1 0.9 %copy-start.2 = (f32[5,4096]{1,0:T(8,128)S(1)}, f32[5,4096]{1,0:T(8,128)}, u32[]{:S(2)}) copy-start(f32[5,4096]{1,0:T(8,128)} %all-reduce.2.cloned.1.call-done) | copy-start | bytes 245764
Sparse Core Ops, SparseCore 0:
  30.9 34.0 all-reduce.1
where the time goes:
time: 75.4 us; the launch traced here: 74.5 us
  starting transfers between devices  22.9 us (30%)
  waiting for transfers between devices  18.3 us (24%)
  between operations  14.6 us (19%)
  other arithmetic  11.3 us (15%)
  local copies, waits for them, and re-layouts  7.48 us (10%)
    ppermute x4, starting transfers between devices, extended(): lax.ppermute(tail, axis, [(i, (i + 1) % count) for i in range(ends)])  17.7 us
    ppermute x4, waiting for transfers between devices, extended(): lax.ppermute(head, axis, [((i + 1) % count, i) for i in range(ends)])  11 us
    psum x1, waiting for transfers between devices, local(): totals = lax.psum(partial_value, 'modes')  7.24 us
    unnamed x31, local copies, waits for them, and re-layouts  5.75 us
    ppermute x4, starting transfers between devices, extended(): lax.ppermute(head, axis, [((i + 1) % count, i) for i in range(ends)])  5.16 us
    add x3, other arithmetic, rate(): left_w + right_w  1.75 us
  transfers between devices with their start and end apart: 9, of which 4 were waited for; matrix products, arithmetic and copies ran while one was open for 10% of the time, Pallas kernels for 0%

commit v1 on v0

v1 whole, which is shorter than its diff:
```python
import functools
import math

import jax
import jax.numpy as jnp
from jax import lax
from jax.experimental import pallas as pl
from jax.experimental.pallas import tpu as pltpu
from jax.sharding import PartitionSpec as P

time_step = 0.6
start_time = 10.0
exchange_coupling = 0.5
LANES = 128
SUBS = 8
STEP_COEF = (time_step / 4.0, time_step / 3.0, time_step / 2.0, time_step)
FIELD_ROWS = 8
PACK_ROWS = 4 * SUBS + FIELD_ROWS


def lane_iota():
    return lax.broadcasted_iota(jnp.int32, (SUBS, LANES), 1)


def sub_iota():
    return lax.broadcasted_iota(jnp.int32, (SUBS, LANES), 0)


def shift_from_left(tile):
    return pltpu.roll(tile, 1, 1)


def shift_from_right(tile):
    return pltpu.roll(tile, LANES - 1, 1)


def column(read):
    rows = sub_iota()
    out = jnp.full((SUBS, LANES), read(0))
    for mode in range(1, SUBS):
        out = jnp.where(rows == mode, read(mode), out)
    return out


def source_terms(parts, masked_cos, masked_sin):
    up_real, down_real, up_imag, down_imag = parts
    return (
        masked_cos * up_real + masked_sin * down_real,
        masked_cos * down_real - masked_sin * up_real,
        masked_cos * up_imag + masked_sin * down_imag,
        masked_cos * down_imag - masked_sin * up_imag,
    )


def horner(base, state, hops, fields, source, coef):
    up_real, down_real, up_imag, down_imag = state
    plus, minus, field_x, field_y = fields
    h_up_real = plus * up_real + field_x * down_real + field_y * down_imag - hops[0] + source[0]
    h_down_real = minus * down_real + field_x * up_real - field_y * up_imag - hops[1] + source[1]
    h_up_imag = plus * up_imag + field_x * down_imag - field_y * down_real - hops[2] + source[2]
    h_down_imag = minus * down_imag + field_x * up_imag + field_y * up_real - hops[3] + source[3]
    return (
        base[0] + coef * h_up_imag,
        base[1] + coef * h_down_imag,
        base[2] - coef * h_up_real,
        base[3] - coef * h_down_real,
    )


def prepare_kernel(
    all_modes,
    wave_ref,
    potential_ref,
    angle_ref,
    magnet_ref,
    mask_ref,
    weight_ref,
    amp_ref,
    group_ref,
    energies_ref,
    lead_ref,
    turned_ref,
    fields_ref,
    payload_ref,
    pack_a_ref,
    pack_b_ref,
    head_ref,
    tail_ref,
    source_ref,
):
    tiles = angle_ref.shape[0]
    lanes = lane_iota()
    site_index = lax.axis_index("sites")
    mode_index = lax.axis_index("modes")

    cosine = jnp.cos(angle_ref[...])
    sine = jnp.sin(angle_ref[...])
    fields_ref[4] = cosine
    fields_ref[5] = sine
    for part in range(3):
        for tile in range(tiles):
            fields_ref[part, tile : tile + 1, :] = magnet_ref[
                part : part + 1, tile * LANES : (tile + 1) * LANES
            ]
    strength = exchange_coupling * mask_ref[...].astype(jnp.float32)
    field_x = strength * fields_ref[0]
    field_y = strength * fields_ref[1]
    field_z = strength * fields_ref[2]
    cos_two = cosine * cosine - sine * sine
    sin_two = 2.0 * (cosine * sine)
    turned_z = field_z * cos_two + field_x * sin_two
    fields_ref[0] = potential_ref[...] + turned_z
    fields_ref[1] = potential_ref[...] - turned_z
    fields_ref[2] = field_x * cos_two - field_z * sin_two
    fields_ref[3] = field_y

    energy = column(lambda mode: energies_ref[group_ref[mode]])
    amps = [column(lambda mode, part=part: amp_ref[part, mode]) for part in range(4)]
    stages = []
    for offset in (0.0, 0.5 * time_step, time_step):
        phase = energy * (start_time + offset)
        cos_phase = jnp.cos(phase)
        sin_phase = jnp.sin(phase)
        stages.append(
            (
                amps[0] * cos_phase + amps[2] * sin_phase,
                amps[1] * cos_phase + amps[3] * sin_phase,
                amps[2] * cos_phase - amps[0] * sin_phase,
                amps[3] * cos_phase - amps[1] * sin_phase,
            )
        )
    first, middle, last = stages
    for part in range(4):
        combined = (
            first[part],
            0.5 * (first[part] + middle[part]),
            (first[part] + 2.0 * middle[part]) * (1.0 / 3.0),
            (first[part] + 4.0 * middle[part] + last[part]) * (1.0 / 6.0),
        )
        for step in range(4):
            source_ref[step * 4 + part] = combined[step]
    source_ref[16] = column(lambda mode: lead_ref[mode].astype(jnp.float32))

    weight = column(lambda mode: weight_ref[mode])
    charge_scale = 1.0 / all_modes
    spin_scale = 1.0 / math.sqrt(all_modes)

    def rotated(tile):
        at = pl.ds(pl.multiple_of(tile * LANES, LANES), LANES)
        cos_row = fields_ref[4, pl.ds(tile, 1), :]
        sin_row = fields_ref[5, pl.ds(tile, 1), :]
        up_real, down_real, up_imag, down_imag = (wave_ref[part, :, at] for part in range(4))
        out = (
            cos_row * up_real + sin_row * down_real,
            cos_row * down_real - sin_row * up_real,
            cos_row * up_imag + sin_row * down_imag,
            cos_row * down_imag - sin_row * up_imag,
        )
        for part in range(4):
            turned_ref[part, :, at] = out[part]
        return out

    def visit(tile, here, here_rolled, after_rolled, inside):
        at = pl.ds(pl.multiple_of(tile * LANES, LANES), LANES)
        up_real, down_real, up_imag, down_imag = (wave_ref[part, :, at] for part in range(4))
        follow = [jnp.where(lanes == LANES - 1, b, a) for a, b in zip(here_rolled, after_rolled)]
        up_square = up_real * up_real + up_imag * up_imag
        down_square = down_real * down_real + down_imag * down_imag
        current = (
            here[0] * follow[2] + here[1] * follow[3] - here[2] * follow[0] - here[3] * follow[1]
        )
        rows = (
            (up_square + down_square, charge_scale),
            (up_real * down_real + up_imag * down_imag, 2.0 * spin_scale),
            (up_real * down_imag - up_imag * down_real, 2.0 * spin_scale),
            (up_square - down_square, spin_scale),
            (current, 2.0 * spin_scale),
        )
        for place, (value, scale) in enumerate(rows):
            payload_ref[pl.ds(place * tiles + tile, 1), :] = scale * jnp.sum(
                value * weight, axis=0, keepdims=True
            )

    def body(tile, carry):
        here, here_rolled = carry
        after = rotated(tile + 1)
        after_rolled = tuple(shift_from_right(x) for x in after)
        visit(tile, here, here_rolled, after_rolled, True)
        return after, after_rolled

    begin = rotated(0)
    here, here_rolled = lax.fori_loop(
        0, tiles - 1, body, (begin, tuple(shift_from_right(x) for x in begin)), unroll=4
    )
    nothing = (jnp.zeros((SUBS, LANES), jnp.float32),) * 4
    visit(tiles - 1, here, here_rolled, nothing, False)

    slot = mode_index * 4
    scaled = (2.0 * spin_scale) * weight
    tails = jnp.zeros((SUBS, LANES), jnp.float32)
    heads = jnp.zeros((SUBS, LANES), jnp.float32)
    final = (tiles - 1) * LANES
    for part in range(4):
        tail_column = turned_ref[part, :, final + LANES - 1 : final + LANES]
        tails = jnp.where(lanes == slot + part, scaled * tail_column, tails)
        head_column = turned_ref[(part + 2) % 4, :, 0:1]
        head_column = head_column if part < 2 else -head_column
        heads = jnp.where(lanes == slot + part, head_column, heads)
    payload_ref[5 * tiles : 5 * tiles + SUBS, :] = tails
    payload_ref[5 * tiles + SUBS : 5 * tiles + 2 * SUBS, :] = heads

    for part in range(4):
        head_ref[part * SUBS : (part + 1) * SUBS, :] = turned_ref[part, :, 0:LANES]
        tail_ref[part * SUBS : (part + 1) * SUBS, :] = turned_ref[part, :, final : final + LANES]
    for part in range(6):
        head_ref[32 + part : 33 + part, :] = fields_ref[part, 0:1, :]
        tail_ref[32 + part : 33 + part, :] = fields_ref[part, tiles - 1 : tiles, :]
    ends = jnp.where(lax.broadcasted_iota(jnp.int32, (2, LANES), 0) == 0, 1.0, 0.0)
    head_ref[38:40, :] = ends
    tail_ref[38:40, :] = ends
    even = lax.rem(site_index, 2) == 0
    pack_a_ref[...] = jnp.where(even, tail_ref[...], head_ref[...])
    pack_b_ref[...] = jnp.where(even, head_ref[...], tail_ref[...])


def region_masks(positions, lead, span, cos_row, sin_row):
    offset = positions - lead
    inside = (offset >= 0.0) & (offset < span)
    zero = jnp.zeros((SUBS, LANES), jnp.float32)
    return jnp.where(inside, cos_row, zero), jnp.where(inside, sin_row, zero)


def interior_kernel(span, turned_ref, fields_ref, source_ref, next_ref, edge_ref, work_ref):
    tiles = fields_ref.shape[1]
    lanes = lane_iota()
    first_site = lax.axis_index("sites") * (tiles * LANES)
    lane_position = (lanes + first_site).astype(jnp.float32)
    lead = source_ref[16]
    zero = (jnp.zeros((SUBS, LANES), jnp.float32),) * 4

    for step in range(4):
        origin_ref = turned_ref if step == 0 else work_ref
        parts = [source_ref[step * 4 + part] for part in range(4)]

        def load(tile, origin_ref=origin_ref):
            at = pl.ds(pl.multiple_of(tile * LANES, LANES), LANES)
            return tuple(origin_ref[part, :, at] for part in range(4))

        def visit(tile, before_up, here, here_up, here_down, after_down, step=step, parts=parts):
            at = pl.ds(pl.multiple_of(tile * LANES, LANES), LANES)
            base = tuple(turned_ref[part, :, at] for part in range(4))
            rows = [fields_ref[place, pl.ds(tile, 1), :] for place in range(6)]
            hops = [
                jnp.where(lanes == 0, b, a) + jnp.where(lanes == LANES - 1, d, c)
                for a, b, c, d in zip(here_up, before_up, here_down, after_down)
            ]
            tile_start = lax.convert_element_type(tile * LANES, jnp.float32)
            masked = region_masks(lane_position + tile_start, lead, span, rows[4], rows[5])
            out = horner(
                base, here, hops, rows[:4], source_terms(parts, *masked), STEP_COEF[step]
            )
            if step == 3:
                out = (
                    rows[4] * out[0] - rows[5] * out[1],
                    rows[5] * out[0] + rows[4] * out[1],
                    rows[4] * out[2] - rows[5] * out[3],
                    rows[5] * out[2] + rows[4] * out[3],
                )
                for part in range(4):
                    next_ref[part, :, at] = out[part]
            else:
                for part in range(4):
                    work_ref[part, :, at] = out[part]

        def body(tile, carry, load=load, visit=visit):
            before_up, here, here_up, here_down = carry
            after = load(tile + 1)
            after_up = tuple(shift_from_left(x) for x in after)
            after_down = tuple(shift_from_right(x) for x in after)
            visit(tile, before_up, here, here_up, here_down, after_down)
            return here_up, after, after_up, after_down

        begin = load(0)
        carry = (
            zero,
            begin,
            tuple(shift_from_left(x) for x in begin),
            tuple(shift_from_right(x) for x in begin),
        )
        carry = lax.fori_loop(0, tiles - 1, body, carry, unroll=2)
        visit(tiles - 1, *carry, zero)

    final = (tiles - 1) * LANES
    for part in range(4):
        edge_ref[part] = next_ref[part, :, 0:LANES]
        edge_ref[4 + part] = next_ref[part, :, final : final + LANES]


def finish_kernel(
    span,
    mode_bits,
    *refs,
):
    (
        interior_ref,
        edge_ref,
        head_ref,
        tail_ref,
        recv_a_ref,
        recv_b_ref,
        source_ref,
        own_ref,
        other_ref,
        beyond_ref,
        beyond_other_ref,
        magnet_ref,
        mask_ref,
        next_ref,
        densities_ref,
        magnet_next_ref,
        patch_ref,
        sems,
    ) = refs
    tiles = mask_ref.shape[0]
    lanes = lane_iota()
    first_site = lax.axis_index("sites") * (tiles * LANES)
    even = lax.rem(lax.axis_index("sites"), 2) == 0
    lead = source_ref[16]
    final = (tiles - 1) * LANES
    half = LANES // 2

    left = jnp.where(even, recv_b_ref[...], recv_a_ref[...])
    right = jnp.where(even, recv_a_ref[...], recv_b_ref[...])
    upper = lax.broadcasted_iota(jnp.int32, (PACK_ROWS, LANES), 1) >= half
    patches = []
    for side, block in enumerate(
        (jnp.where(upper, left, head_ref[...]), jnp.where(upper, tail_ref[...], right))
    ):
        base = tuple(block[part * SUBS : (part + 1) * SUBS, :] for part in range(4))
        rows = [block[32 + place : 33 + place, :] for place in range(7)]
        if side == 0:
            position = first_site + jnp.where(lanes >= half, lanes - LANES, lanes)
        else:
            position = first_site + final + jnp.where(lanes >= half, lanes, lanes + LANES)
        masked = region_masks(position.astype(jnp.float32), lead, span, rows[4], rows[5])
        state = base
        for step in range(4):
            parts = [source_ref[step * 4 + part] for part in range(4)]
            hops = [shift_from_left(x) + shift_from_right(x) for x in state]
            state = horner(base, state, hops, rows[:4], source_terms(parts, *masked), STEP_COEF[step])
            state = tuple(rows[6] * x for x in state)
        out = (
            rows[4] * state[0] - rows[5] * state[1],
            rows[5] * state[0] + rows[4] * state[1],
            rows[4] * state[2] - rows[5] * state[3],
            rows[5] * state[2] + rows[4] * state[3],
        )
        fresh = lanes < 4 if side == 0 else lanes >= LANES - 4
        for part in range(4):
            patch_ref[side, part] = jnp.where(fresh, out[part], edge_ref[side * 4 + part])
    copies = [
        pltpu.make_async_copy(
            patch_ref.at[side],
            next_ref.at[:, :, pl.ds(side * final, LANES)],
            sems.at[side],
        )
        for side in range(2)
    ]
    for copy in copies:
        copy.start()

    for place in range(5):
        rows = pl.ds(place * tiles, tiles)
        total = own_ref[rows, :] + other_ref[rows, :]
        if place == 4:
            ends = pl.ds(5 * tiles, SUBS)
            tails = own_ref[ends, :] + other_ref[ends, :]
            heads = beyond_ref[...] + beyond_other_ref[...]
            corner = jnp.sum(jnp.sum(tails * heads, axis=1, keepdims=True), axis=0, keepdims=True)
            row_at = lax.broadcasted_iota(jnp.int32, (tiles, LANES), 0)
            lane_at = lax.broadcasted_iota(jnp.int32, (tiles, LANES), 1)
            total = jnp.where((row_at == tiles - 1) & (lane_at == LANES - 1), corner, total)
        for tile in range(tiles):
            densities_ref[place : place + 1, tile * LANES : (tile + 1) * LANES] = total[
                tile : tile + 1, :
            ]
    for tile in range(tiles):
        at = slice(tile * LANES, (tile + 1) * LANES)
        mask_row = mask_ref[tile : tile + 1, :].astype(jnp.float32)
        field_x, field_y, field_z = (
            exchange_coupling * densities_ref[1 + part : 2 + part, at] for part in range(3)
        )
        magnet_x, magnet_y, magnet_z = (magnet_ref[part : part + 1, at] for part in range(3))
        torque = (
            magnet_y * field_z - magnet_z * field_y,
            magnet_z * field_x - magnet_x * field_z,
            magnet_x * field_y - magnet_y * field_x,
        )
        for part, magnet in enumerate((magnet_x, magnet_y, magnet_z)):
            magnet_next_ref[part : part + 1, at] = magnet - time_step * (mask_row * torque[part])

    for copy in copies:
        copy.wait()


def local(
    wave_state,
    potential,
    spin_angle,
    magnet,
    magnetic_mask,
    mode_weight,
    source_amp,
    mode_group,
    energies,
    lead_site,
):
    local_modes, local_sites = wave_state.shape[1:]
    site_count = lax.axis_size("sites")
    mode_count = lax.axis_size("modes")
    assert local_modes == SUBS and local_sites % LANES == 0
    tiles = local_sites // LANES
    span = float(local_sites * site_count // 8)
    f32 = jnp.float32
    vmem = pl.BlockSpec(memory_space=pltpu.VMEM)
    smem = pl.BlockSpec(memory_space=pltpu.SMEM)
    anywhere = pl.BlockSpec(memory_space=pl.ANY)
    dense = (tiles, LANES)
    payload_rows = 5 * tiles + 2 * SUBS

    turned, fields, payload, pack_a, pack_b, head, tail, source = pl.pallas_call(
        functools.partial(prepare_kernel, local_modes * mode_count),
        out_shape=(
            jax.ShapeDtypeStruct(wave_state.shape, f32),
            jax.ShapeDtypeStruct((6,) + dense, f32),
            jax.ShapeDtypeStruct((payload_rows, LANES), f32),
            jax.ShapeDtypeStruct((PACK_ROWS, LANES), f32),
            jax.ShapeDtypeStruct((PACK_ROWS, LANES), f32),
            jax.ShapeDtypeStruct((PACK_ROWS, LANES), f32),
            jax.ShapeDtypeStruct((PACK_ROWS, LANES), f32),
            jax.ShapeDtypeStruct((17, SUBS, LANES), f32),
        ),
        in_specs=[vmem] * 5 + [smem] * 5,
        out_specs=[vmem] * 8,
        name="prepare",
        cost_estimate=pl.CostEstimate(flops=10_000_000, bytes_accessed=1_500_000, transcendentals=0),
    )(
        wave_state,
        potential.reshape(dense),
        spin_angle.reshape(dense),
        magnet,
        magnetic_mask.reshape(dense),
        mode_weight,
        source_amp,
        mode_group,
        energies,
        lead_site,
    )

    pairs_a = [(i, i + 1) for i in range(0, site_count - 1, 2)]
    pairs_b = [(i, i + 1) for i in range(1, site_count - 1, 2)]
    both = lambda pairs: pairs + [(j, i) for i, j in pairs]
    recv_b = lax.ppermute(pack_b, "sites", both(pairs_b))
    recv_a = lax.ppermute(pack_a, "sites", both(pairs_a))

    own = payload
    distance = 1
    while 2 * distance < mode_count:
        own = own + lax.ppermute(own, "modes", [(i, i ^ distance) for i in range(mode_count)])
        distance *= 2
    other = lax.ppermute(own, "modes", [(i, i ^ distance) for i in range(mode_count)])

    heads = slice(5 * tiles + SUBS, payload_rows)
    to_left = [(i + 1, i) for i in range(site_count - 1)]
    beyond = lax.ppermute(own[heads] + other[heads], "sites", to_left)
    beyond_other = jnp.zeros_like(beyond)

    interior, edge = pl.pallas_call(
        functools.partial(interior_kernel, span),
        out_shape=(
            jax.ShapeDtypeStruct(wave_state.shape, f32),
            jax.ShapeDtypeStruct((8, SUBS, LANES), f32),
        ),
        in_specs=[vmem] * 3,
        out_specs=[vmem] * 2,
        scratch_shapes=[pltpu.VMEM(wave_state.shape, f32)],
        name="interior",
        cost_estimate=pl.CostEstimate(flops=20_000_000, bytes_accessed=1_500_000, transcendentals=0),
    )(turned, fields, source)

    next_state, densities, magnet_next = pl.pallas_call(
        functools.partial(finish_kernel, span, mode_count),
        out_shape=(
            jax.ShapeDtypeStruct(wave_state.shape, f32),
            jax.ShapeDtypeStruct((5, local_sites), f32),
            jax.ShapeDtypeStruct((3, local_sites), f32),
        ),
        in_specs=[anywhere] + [vmem] * 12,
        out_specs=[anywhere, vmem, vmem],
        scratch_shapes=[
            pltpu.VMEM((2, 4, SUBS, LANES), f32),
            pltpu.SemaphoreType.DMA((2,)),
        ],
        input_output_aliases={0: 0},
        name="finish",
        cost_estimate=pl.CostEstimate(flops=1_000_000, bytes_accessed=400_000, transcendentals=0),
    )(
        interior,
        edge,
        head,
        tail,
        recv_a,
        recv_b,
        source,
        own,
        other,
        beyond,
        beyond_other,
        magnet,
        magnetic_mask.reshape(dense),
    )
    return (next_state, densities, magnet_next)


def solution(mesh):
    return jax.shard_map(
        local,
        mesh=mesh,
        in_specs=(
            P(None, "modes", "sites"),
            P("sites"),
            P("sites"),
            P(None, "sites"),
            P("sites"),
            P("modes"),
            P(None, "modes"),
            P("modes"),
            P(),
            P("modes"),
        ),
        out_specs=(P(None, "modes", "sites"), P(None, "sites"), P(None, "sites")),
        check_vma=False,
    )
```

time: 75.4 us -> 29.7 us (0.39)
  the two profiles are of different devices: /device:TPU:0 before, /device:TPU:8 now
where the time goes in v1:
time: 29.7 us; the launch traced here: 29.5 us
  Pallas kernels  15.8 us (53%)
  starting transfers between devices  9.88 us (33%)
  waiting for transfers between devices  1.5 us (5%)
  other arithmetic  0.91 us (3%)
  between operations  0.76 us (3%)
  local copies, waits for them, and re-layouts  0.62 us (2%)
    pallas_call x1, Pallas kernels, local(): pl.pallas_call(functools.partial(interior_kernel, span), out_shape=(jax.S...  9.72 us
    ppermute x1, starting transfers between devices, local(): beyond = lax.ppermute(own[heads] + other[heads], 'sites', to_left)  4.41 us
    pallas_call x1, Pallas kernels, local(): pl.pallas_call(functools.partial(prepare_kernel, local_modes * mode_count...  3.23 us
    pallas_call x1, Pallas kernels, local(): pl.pallas_call(functools.partial(finish_kernel, span, mode_count), out_sh...  2.84 us
    ppermute x1, starting transfers between devices, local(): recv_b = lax.ppermute(pack_b, 'sites', both(pairs_b))  2.32 us
    ppermute x2, starting transfers between devices, local(): lax.ppermute(own, 'modes', [(i, i ^ distance) for i in range(mode_count)])  1.66 us
    ppermute x1, starting transfers between devices, local(): recv_a = lax.ppermute(pack_a, 'sites', both(pairs_a))  1.49 us
    ppermute x2, waiting for transfers between devices, local(): lax.ppermute(own, 'modes', [(i, i ^ distance) for i in range(mode_count)])  1.49 us
  transfers between devices with their start and end apart: 5, of which 1 were waited for; matrix products, arithmetic and copies ran while one was open for 0% of the time, Pallas kernels for 33%

profile of v1, /device:TPU:8, one launch (start us, length us, event | category | flops | bytes accessed | tf_op | source)
XLA Modules:
  0.0 29.5 jit_solution(6632904392111591525)
XLA Ops:
  0.6 3.2 %prepare.1 = (f32[4,8,4096]{2,1,0:T(8,128)}, f32[6,32,128]{2,1,0:T(8,128)}, f32[176,128]{1,0:T(8,128)}, f32[40,128]{1,0:T(8,128)}, f32[40,128]{1,0:T(8,128)}, /*...) custom-call(f32[4,8,4096]{2,1,0:T(8,128)} %wave_ref.1, f32[32,128]{1,0:T(8,128)} %bitcast.5, ...), custom_call_target="tpu_custom_call" | custom-call | flops 10000000 | bytes 1500000 | tf_op jit(solution)/shard_map/prepare/pallas_call | solution.py:431
  3.9 0.0 copy-start.6
  3.9 0.0 copy-start.5
  3.9 0.1 collective-permute-start.2
  4.0 1.5 %collective-permute-done.2 = f32[176,128]{1,0:T(8,128)S(1)} collective-permute-done((f32[176,128]{1,0:T(8,128)}, f32[176,128]{1,0:T(8,128)S(1)}, u32[]{:S(2)}, u32[]{:S(2)}) %collective-permute-start.2) | collective-permute-done | bytes 90144 | tf_op jit(solution)/shard_map/ppermute | solution.py:469
  5.5 0.9 %add.6.refs_7_ = f32[176,128]{1,0:T(8,128)S(1)} add(f32[176,128]{1,0:T(8,128)} %get-tuple-element.22, f32[176,128]{1,0:T(8,128)S(1)} %collective-permute-done.2) | non-fusion elementwise | flops 22528 | bytes 270336 | tf_op jit(solution)/shard_map/add | solution.py:469
  6.4 0.0 copy-start
  6.4 1.6 %collective-permute-start.3 = (f32[176,128]{1,0:T(8,128)S(1)}, f32[176,128]{1,0:T(8,128)S(1)}, u32[]{:S(2)}, u32[]{:S(2)}) collective-permute-start(f32[176,128]{1,0:T(8,128)S(1)} %add.6.refs_7_), channel_id=1, source_target_pairs={{0,16},{8,24},{16,0},{24,8},{1,17},{9,25},{17,1},{25,9},{2,18},{10... | collective-permute-start | bytes 270344 | tf_op jit(solution)/shard_map/ppermute | solution.py:471
  8.0 0.0 copy-done.6
  8.0 1.5 %collective-permute-start = (f32[40,128]{1,0:T(8,128)S(1)}, f32[40,128]{1,0:T(8,128)S(1)}, u32[]{:S(2)}, u32[]{:S(2)}) collective-permute-start(f32[40,128]{1,0:T(8,128)S(1)} %copy-done.6), channel_id=1, source_target_pairs={{0,1},{2,3},{4,5},{6,7},{1,0},{3,2},{5,4},{7,6},{8,9},{10,11},{12,... | collective-permute-start | bytes 61448 | tf_op jit(solution)/shard_map/ppermute | solution.py:464
  9.5 0.0 copy-done.5
  9.5 2.3 %collective-permute-start.1 = (f32[40,128]{1,0:T(8,128)S(1)}, f32[40,128]{1,0:T(8,128)S(1)}, u32[]{:S(2)}, u32[]{:S(2)}) collective-permute-start(f32[40,128]{1,0:T(8,128)S(1)} %copy-done.5), channel_id=1, source_target_pairs={{1,2},{3,4},{5,6},{2,1},{4,3},{6,5},{9,10},{11,12},{13,14},{10,9},... | collective-permute-start | bytes 61448 | tf_op jit(solution)/shard_map/ppermute | solution.py:463
  11.8 0.0 collective-permute-done.3.refs_8_
  11.8 0.0 copy-start.1
  11.8 4.4 %collective-permute-start.4 = (f32[8,128]{1,0:T(8,128)S(1)}, f32[8,128]{1,0:T(8,128)S(1)}, u32[]{:S(2)}, u32[]{:S(2)}) collective-permute-start(f32[8,128]{1,0:T(8,128)S(1)} %slice_add_fusion), channel_id=1, source_target_pairs={{1,0},{2,1},{3,2},{4,3},{5,4},{6,5},{7,6},{9,8},{10,9},{11,10},{12... | collective-permute-start | bytes 12296 | tf_op jit(solution)/shard_map/ppermute | solution.py:475
  16.2 9.7 %interior.1 = (f32[4,8,4096]{2,1,0:T(8,128)}, f32[8,8,128]{2,1,0:T(8,128)}) custom-call(f32[4,8,4096]{2,1,0:T(8,128)} %get-tuple-element.13.turned_ref, f32[6,32,128]{2,1,0:T(8,128)} %get-tuple-element.14.fields_ref, f32[17,8,128]{2,1,0:T(8,128)} %get-tuple-element.15.source_ref.refs_6_), custom_call_target="tpu_custom_call" | custom-call | flops 20000000 | bytes 1500000 | tf_op jit(solution)/shard_map/interior/pallas_call | solution.py:478
  26.0 0.0 copy-done
  26.0 0.0 copy-done.1
  26.0 0.0 collective-permute-done.refs_4_
  26.0 0.0 copy-start.2
  26.0 0.0 collective-permute-done.1.refs_5_
  26.0 0.0 copy-start.3
  26.0 0.0 collective-permute-done.4.refs_9_
  26.0 0.0 copy-start.4
  26.0 0.6 %broadcast_in_dim.3.refs_10_ = f32[8,128]{1,0:T(8,128)} broadcast(f32[]{:T(128)} %constant.0.clone.1), dimensions={} | broadcast | bytes 4100 | tf_op jit(solution)/shard_map/broadcast_in_dim | solution.py:476
  26.6 0.0 copy-done.2
  26.6 0.0 copy-done.3
  26.6 0.0 copy-done.4
  26.6 2.8 %finish.1 = (f32[4,8,4096]{2,1,0:T(8,128)}, f32[5,4096]{1,0:T(8,128)}, f32[3,4096]{1,0:T(4,128)}) custom-call(f32[4,8,4096]{2,1,0:T(8,128)} %get-tuple-element.16.refs_0_, f32[8,8,128]{2,1,0:T(8,128)} %get-tuple-element.17.refs_1_, f32[40,128]{1,0:T(8,128)} %get-tuple-element.18.refs_2_, ...), custom_call_target="tpu_custom_call", output_to_operand_aliasing={{0}: (0, {})} | custom-call | flops 1000000 | bytes 400000 | tf_op jit(solution)/shard_map/finish/pallas_call | solution.py:491
  (1 shorter events, 0.0 us)
Async XLA Ops:
  3.9 4.1 %copy-start.6 = (f32[40,128]{1,0:T(8,128)S(1)}, f32[40,128]{1,0:T(8,128)}, u32[]{:S(2)}) copy-start(f32[40,128]{1,0:T(8,128)} %get-tuple-element.20) | copy-start | bytes 61444
  3.9 5.6 %copy-start.5 = (f32[40,128]{1,0:T(8,128)S(1)}, f32[40,128]{1,0:T(8,128)}, u32[]{:S(2)}) copy-start(f32[40,128]{1,0:T(8,128)} %get-tuple-element.21) | copy-start | bytes 61444
  3.9 1.6 %collective-permute-start.2 = (f32[176,128]{1,0:T(8,128)}, f32[176,128]{1,0:T(8,128)S(1)}, u32[]{:S(2)}, u32[]{:S(2)}) collective-permute-start(f32[176,128]{1,0:T(8,128)} %get-tuple-element.22), channel_id=1, source_target_pairs={{0,8},{8,0},{16,24},{24,16},{1,9},{9,1},{17,25},{25,17},{2,10},{10... | collective-permute-start | bytes 270344 | tf_op jit(solution)/shard_map/ppermute | solution.py:469
  6.4 19.6 %copy-start = (f32[176,128]{1,0:T(8,128)}, f32[176,128]{1,0:T(8,128)S(1)}, u32[]{:S(2)}) copy-start(f32[176,128]{1,0:T(8,128)S(1)} %add.6.refs_7_) | copy-start | bytes 270340
  6.4 5.4 %collective-permute-start.3 = (f32[176,128]{1,0:T(8,128)S(1)}, f32[176,128]{1,0:T(8,128)S(1)}, u32[]{:S(2)}, u32[]{:S(2)}) collective-permute-start(f32[176,128]{1,0:T(8,128)S(1)} %add.6.refs_7_), channel_id=1, source_target_pairs={{0,16},{8,24},{16,0},{24,8},{1,17},{9,25},{17,1},{25,9},{2,18},{10... | collective-permute-start | bytes 270344 | tf_op jit(solution)/shard_map/ppermute | solution.py:471
  8.0 18.0 %collective-permute-start = (f32[40,128]{1,0:T(8,128)S(1)}, f32[40,128]{1,0:T(8,128)S(1)}, u32[]{:S(2)}, u32[]{:S(2)}) collective-permute-start(f32[40,128]{1,0:T(8,128)S(1)} %copy-done.6), channel_id=1, source_target_pairs={{0,1},{2,3},{4,5},{6,7},{1,0},{3,2},{5,4},{7,6},{8,9},{10,11},{12,... | collective-permute-start | bytes 61448 | tf_op jit(solution)/shard_map/ppermute | solution.py:464
  9.5 16.5 %collective-permute-start.1 = (f32[40,128]{1,0:T(8,128)S(1)}, f32[40,128]{1,0:T(8,128)S(1)}, u32[]{:S(2)}, u32[]{:S(2)}) collective-permute-start(f32[40,128]{1,0:T(8,128)S(1)} %copy-done.5), channel_id=1, source_target_pairs={{1,2},{3,4},{5,6},{2,1},{4,3},{6,5},{9,10},{11,12},{13,14},{10,9},... | collective-permute-start | bytes 61448 | tf_op jit(solution)/shard_map/ppermute | solution.py:463
  11.8 14.2 %copy-start.1 = (f32[176,128]{1,0:T(8,128)}, f32[176,128]{1,0:T(8,128)S(1)}, u32[]{:S(2)}) copy-start(f32[176,128]{1,0:T(8,128)S(1)} %collective-permute-done.3.refs_8_) | copy-start | bytes 270340
  11.8 14.2 %collective-permute-start.4 = (f32[8,128]{1,0:T(8,128)S(1)}, f32[8,128]{1,0:T(8,128)S(1)}, u32[]{:S(2)}, u32[]{:S(2)}) collective-permute-start(f32[8,128]{1,0:T(8,128)S(1)} %slice_add_fusion), channel_id=1, source_target_pairs={{1,0},{2,1},{3,2},{4,3},{5,4},{6,5},{7,6},{9,8},{10,9},{11,10},{12... | collective-permute-start | bytes 12296 | tf_op jit(solution)/shard_map/ppermute | solution.py:475
  26.0 0.6 %copy-start.2 = (f32[40,128]{1,0:T(8,128)}, f32[40,128]{1,0:T(8,128)S(1)}, u32[]{:S(2)}) copy-start(f32[40,128]{1,0:T(8,128)S(1)} %collective-permute-done.refs_4_) | copy-start | bytes 61444
  26.0 0.6 %copy-start.3 = (f32[40,128]{1,0:T(8,128)}, f32[40,128]{1,0:T(8,128)S(1)}, u32[]{:S(2)}) copy-start(f32[40,128]{1,0:T(8,128)S(1)} %collective-permute-done.1.refs_5_) | copy-start | bytes 61444
  26.0 0.6 %copy-start.4 = (f32[8,128]{1,0:T(8,128)}, f32[8,128]{1,0:T(8,128)S(1)}, u32[]{:S(2)}) copy-start(f32[8,128]{1,0:T(8,128)S(1)} %collective-permute-done.4.refs_9_) | copy-start | bytes 12292

commit v2 on v1

v2 whole, which is shorter than its diff:
```python
import functools
import math

import jax
import jax.numpy as jnp
from jax import lax
from jax.experimental import pallas as pl
from jax.experimental.pallas import tpu as pltpu
from jax.sharding import PartitionSpec as P

time_step = 0.6
start_time = 10.0
exchange_coupling = 0.5
LANES = 128
SUBS = 8
PIECES = 4
STEP_COEF = (time_step / 4.0, time_step / 3.0, time_step / 2.0, time_step)
FIELD_ROWS = 8
PACK_ROWS = 4 * SUBS + FIELD_ROWS


def lane_iota():
    return lax.broadcasted_iota(jnp.int32, (SUBS, LANES), 1)


def sub_iota():
    return lax.broadcasted_iota(jnp.int32, (SUBS, LANES), 0)


def shift_from_left(tile):
    return pltpu.roll(tile, 1, 1)


def shift_from_right(tile):
    return pltpu.roll(tile, LANES - 1, 1)


def column(read):
    rows = sub_iota()
    out = jnp.full((SUBS, LANES), read(0))
    for mode in range(1, SUBS):
        out = jnp.where(rows == mode, read(mode), out)
    return out


def source_terms(parts, masked_cos, masked_sin):
    up_real, down_real, up_imag, down_imag = parts
    return (
        masked_cos * up_real + masked_sin * down_real,
        masked_cos * down_real - masked_sin * up_real,
        masked_cos * up_imag + masked_sin * down_imag,
        masked_cos * down_imag - masked_sin * up_imag,
    )


def rotate_fore(state, cos_row, sin_row):
    return (
        cos_row * state[0] - sin_row * state[1],
        sin_row * state[0] + cos_row * state[1],
        cos_row * state[2] - sin_row * state[3],
        sin_row * state[2] + cos_row * state[3],
    )


def horner(base, state, hops, fields, source, coef):
    up_real, down_real, up_imag, down_imag = state
    plus, minus, field_x, field_y = fields
    h_up_real = plus * up_real + field_x * down_real + field_y * down_imag - hops[0] + source[0]
    h_down_real = minus * down_real + field_x * up_real - field_y * up_imag - hops[1] + source[1]
    h_up_imag = plus * up_imag + field_x * down_imag - field_y * down_real - hops[2] + source[2]
    h_down_imag = minus * down_imag + field_x * up_imag + field_y * up_real - hops[3] + source[3]
    return (
        base[0] + coef * h_up_imag,
        base[1] + coef * h_down_imag,
        base[2] - coef * h_up_real,
        base[3] - coef * h_down_real,
    )


def prepare_kernel(
    all_modes,
    wave_ref,
    potential_ref,
    angle_ref,
    magnet_ref,
    mask_ref,
    weight_ref,
    amp_ref,
    group_ref,
    energies_ref,
    lead_ref,
    turned_ref,
    fields_ref,
    payload_ref,
    pack_a_ref,
    pack_b_ref,
    source_ref,
    spin_ref,
    wave_in,
    sems,
):
    tiles = angle_ref.shape[0]
    piece = tiles * LANES // PIECES
    copies = [
        pltpu.make_async_copy(
            wave_ref.at[:, :, pl.ds(part * piece, piece)],
            wave_in.at[:, :, pl.ds(part * piece, piece)],
            sems.at[part],
        )
        for part in range(PIECES)
    ]
    for copy in copies:
        copy.start()

    lanes = lane_iota()
    site_index = lax.axis_index("sites")
    mode_index = lax.axis_index("modes")

    cosine = jnp.cos(angle_ref[...])
    sine = jnp.sin(angle_ref[...])
    fields_ref[4] = cosine
    fields_ref[5] = sine
    for part in range(3):
        for tile in range(tiles):
            spin_ref[part, tile : tile + 1, :] = magnet_ref[
                part : part + 1, tile * LANES : (tile + 1) * LANES
            ]
    mask = mask_ref[...].astype(jnp.float32)
    strength = exchange_coupling * mask
    field_x = strength * spin_ref[0]
    field_y = strength * spin_ref[1]
    field_z = strength * spin_ref[2]
    cos_two = cosine * cosine - sine * sine
    sin_two = 2.0 * (cosine * sine)
    turned_z = field_z * cos_two + field_x * sin_two
    fields_ref[0] = potential_ref[...] + turned_z
    fields_ref[1] = potential_ref[...] - turned_z
    fields_ref[2] = field_x * cos_two - field_z * sin_two
    fields_ref[3] = field_y
    spin_ref[3] = time_step * mask

    energy = column(lambda mode: energies_ref[group_ref[mode]])
    amps = [column(lambda mode, part=part: amp_ref[part, mode]) for part in range(4)]
    stages = []
    for offset in (0.0, 0.5 * time_step, time_step):
        phase = energy * (start_time + offset)
        cos_phase = jnp.cos(phase)
        sin_phase = jnp.sin(phase)
        stages.append(
            (
                amps[0] * cos_phase + amps[2] * sin_phase,
                amps[1] * cos_phase + amps[3] * sin_phase,
                amps[2] * cos_phase - amps[0] * sin_phase,
                amps[3] * cos_phase - amps[1] * sin_phase,
            )
        )
    first, middle, last = stages
    for part in range(4):
        combined = (
            first[part],
            0.5 * (first[part] + middle[part]),
            (first[part] + 2.0 * middle[part]) * (1.0 / 3.0),
            (first[part] + 4.0 * middle[part] + last[part]) * (1.0 / 6.0),
        )
        for step in range(4):
            source_ref[step * 4 + part] = combined[step]
    source_ref[16] = column(lambda mode: lead_ref[mode].astype(jnp.float32))

    weight = column(lambda mode: weight_ref[mode])
    charge_scale = 1.0 / all_modes
    spin_scale = 1.0 / math.sqrt(all_modes)
    nothing = (jnp.zeros((SUBS, LANES), jnp.float32),) * 4

    def rotated(tile):
        if tile == tiles:
            return nothing
        at = slice(tile * LANES, (tile + 1) * LANES)
        if tile * LANES % piece == 0:
            copies[tile * LANES // piece].wait()
        cos_row = fields_ref[4, tile : tile + 1, :]
        sin_row = fields_ref[5, tile : tile + 1, :]
        up_real, down_real, up_imag, down_imag = (wave_in[part, :, at] for part in range(4))
        out = (
            cos_row * up_real + sin_row * down_real,
            cos_row * down_real - sin_row * up_real,
            cos_row * up_imag + sin_row * down_imag,
            cos_row * down_imag - sin_row * up_imag,
        )
        for part in range(4):
            turned_ref[part, :, at] = out[part]
        return out

    here = rotated(0)
    here_rolled = [shift_from_right(x) for x in here]
    for tile in range(tiles):
        at = slice(tile * LANES, (tile + 1) * LANES)
        after = rotated(tile + 1)
        after_rolled = [shift_from_right(x) for x in after]
        up_real, down_real, up_imag, down_imag = (wave_in[part, :, at] for part in range(4))
        follow = [jnp.where(lanes == LANES - 1, b, a) for a, b in zip(here_rolled, after_rolled)]
        up_square = up_real * up_real + up_imag * up_imag
        down_square = down_real * down_real + down_imag * down_imag
        current = (
            here[0] * follow[2] + here[1] * follow[3] - here[2] * follow[0] - here[3] * follow[1]
        )
        rows = (
            (up_square + down_square, charge_scale),
            (up_real * down_real + up_imag * down_imag, 2.0 * spin_scale),
            (up_real * down_imag - up_imag * down_real, 2.0 * spin_scale),
            (up_square - down_square, spin_scale),
            (current, 2.0 * spin_scale),
        )
        for place, (value, scale) in enumerate(rows):
            payload_ref[place * tiles + tile : place * tiles + tile + 1, :] = scale * jnp.sum(
                value * weight, axis=0, keepdims=True
            )
        here, here_rolled = after, after_rolled

    slot = mode_index * 4
    scaled = (2.0 * spin_scale) * weight
    tails = jnp.zeros((SUBS, LANES), jnp.float32)
    heads = jnp.zeros((SUBS, LANES), jnp.float32)
    final = (tiles - 1) * LANES
    for part in range(4):
        tail_column = turned_ref[part, :, final + LANES - 1 : final + LANES]
        tails = jnp.where(lanes == slot + part, scaled * tail_column, tails)
        head_column = turned_ref[(part + 2) % 4, :, 0:1]
        head_column = head_column if part < 2 else -head_column
        heads = jnp.where(lanes == slot + part, head_column, heads)
    payload_ref[5 * tiles : 5 * tiles + SUBS, :] = tails
    payload_ref[5 * tiles + SUBS : 5 * tiles + 2 * SUBS, :] = heads

    even = lax.rem(site_index, 2) == 0
    for part in range(4):
        at = slice(part * SUBS, (part + 1) * SUBS)
        head = turned_ref[part, :, 0:LANES]
        tail = turned_ref[part, :, final : final + LANES]
        pack_a_ref[at, :] = jnp.where(even, tail, head)
        pack_b_ref[at, :] = jnp.where(even, head, tail)
    for place in range(6):
        at = slice(32 + place, 33 + place)
        head = fields_ref[place, 0:1, :]
        tail = fields_ref[place, tiles - 1 : tiles, :]
        pack_a_ref[at, :] = jnp.where(even, tail, head)
        pack_b_ref[at, :] = jnp.where(even, head, tail)
    ends = jnp.where(lax.broadcasted_iota(jnp.int32, (2, LANES), 0) == 0, 1.0, 0.0)
    pack_a_ref[38:40, :] = ends
    pack_b_ref[38:40, :] = ends


def region_masks(positions, lead, span, cos_row, sin_row):
    offset = positions - lead
    inside = (offset >= 0.0) & (offset < span)
    zero = jnp.zeros((SUBS, LANES), jnp.float32)
    return jnp.where(inside, cos_row, zero), jnp.where(inside, sin_row, zero)


def interior_kernel(span, turned_ref, fields_ref, source_ref, next_ref, edge_ref, *scratch):
    (work_a, work_b, out_ref, sems) = scratch
    tiles = fields_ref.shape[1]
    piece = tiles * LANES // PIECES
    lanes = lane_iota()
    first_site = lax.axis_index("sites") * (tiles * LANES)
    lane_position = (lanes + first_site).astype(jnp.float32)
    lead = source_ref[16]
    zero = (jnp.zeros((SUBS, LANES), jnp.float32),) * 4
    targets = (work_a, work_b, work_a, out_ref)
    copies = [
        pltpu.make_async_copy(
            out_ref.at[:, :, pl.ds(part * piece, piece)],
            next_ref.at[:, :, pl.ds(part * piece, piece)],
            sems.at[part],
        )
        for part in range(PIECES)
    ]

    for step in range(4):
        origin_ref = turned_ref if step == 0 else targets[step - 1]
        target_ref = targets[step]
        parts = [source_ref[step * 4 + part] for part in range(4)]

        def load(tile):
            if tile == tiles:
                return zero
            return tuple(
                origin_ref[part, :, tile * LANES : (tile + 1) * LANES] for part in range(4)
            )

        before_up = zero
        here = load(0)
        here_up = [shift_from_left(x) for x in here]
        here_down = [shift_from_right(x) for x in here]
        for tile in range(tiles):
            at = slice(tile * LANES, (tile + 1) * LANES)
            after = load(tile + 1)
            after_up = [shift_from_left(x) for x in after]
            after_down = [shift_from_right(x) for x in after]
            base = tuple(turned_ref[part, :, at] for part in range(4))
            rows = [fields_ref[place, tile : tile + 1, :] for place in range(6)]
            hops = [
                jnp.where(lanes == 0, b, a) + jnp.where(lanes == LANES - 1, d, c)
                for a, b, c, d in zip(here_up, before_up, here_down, after_down)
            ]
            masked = region_masks(
                lane_position + float(tile * LANES), lead, span, rows[4], rows[5]
            )
            out = horner(
                base, here, hops, rows[:4], source_terms(parts, *masked), STEP_COEF[step]
            )
            if step == 3:
                out = rotate_fore(out, rows[4], rows[5])
            for part in range(4):
                target_ref[part, :, at] = out[part]
            if step == 3 and (tile + 1) * LANES % piece == 0:
                copies[tile * LANES // piece].start()
            before_up, here, here_up, here_down = here_up, after, after_up, after_down

    final = (tiles - 1) * LANES
    for part in range(4):
        edge_ref[part] = out_ref[part, :, 0:LANES]
        edge_ref[4 + part] = out_ref[part, :, final : final + LANES]
    for copy in copies:
        copy.wait()


def finish_kernel(span, *refs):
    (
        interior_ref,
        edge_ref,
        turned_ref,
        fields_ref,
        recv_a_ref,
        recv_b_ref,
        source_ref,
        own_ref,
        other_ref,
        beyond_ref,
        beyond_other_ref,
        spin_ref,
        next_ref,
        densities_ref,
        magnet_next_ref,
        patch_ref,
        sems,
    ) = refs
    tiles = fields_ref.shape[1]
    lanes = lane_iota()
    first_site = lax.axis_index("sites") * (tiles * LANES)
    even = lax.rem(lax.axis_index("sites"), 2) == 0
    lead = source_ref[16]
    final = (tiles - 1) * LANES
    half = LANES // 2
    upper = lanes >= half
    upper_row = upper[0:1, :]

    for side in range(2):
        near, far = (recv_b_ref, recv_a_ref) if side == 0 else (recv_a_ref, recv_b_ref)

        def joined(pack_at, own, upper_half):
            fetched = jnp.where(even, near[pack_at, :], far[pack_at, :])
            if side == 0:
                return jnp.where(upper_half, fetched, own)
            return jnp.where(upper_half, own, fetched)

        edge_tile = 0 if side == 0 else tiles - 1
        at = slice(edge_tile * LANES, (edge_tile + 1) * LANES)
        base = tuple(
            joined(slice(part * SUBS, (part + 1) * SUBS), turned_ref[part, :, at], upper)
            for part in range(4)
        )
        rows = [
            joined(
                slice(32 + place, 33 + place),
                fields_ref[place, edge_tile : edge_tile + 1, :],
                upper_row,
            )
            for place in range(6)
        ]
        inside = joined(slice(38, 39), jnp.ones((1, LANES), jnp.float32), upper_row)
        if side == 0:
            position = first_site + jnp.where(upper, lanes - LANES, lanes)
        else:
            position = first_site + final + jnp.where(upper, lanes, lanes + LANES)
        masked = region_masks(position.astype(jnp.float32), lead, span, rows[4], rows[5])
        state = base
        for step in range(4):
            parts = [source_ref[step * 4 + part] for part in range(4)]
            hops = [shift_from_left(x) + shift_from_right(x) for x in state]
            state = horner(base, state, hops, rows[:4], source_terms(parts, *masked), STEP_COEF[step])
            if step < 3:
                state = tuple(inside * x for x in state)
        out = rotate_fore(state, rows[4], rows[5])
        fresh = lanes < 4 if side == 0 else lanes >= LANES - 4
        for part in range(4):
            patch_ref[side, part] = jnp.where(fresh, out[part], edge_ref[side * 4 + part])
    copies = [
        pltpu.make_async_copy(
            patch_ref.at[side],
            next_ref.at[:, :, pl.ds(side * final, LANES)],
            sems.at[side],
        )
        for side in range(2)
    ]
    for copy in copies:
        copy.start()

    totals = []
    for place in range(5):
        rows = slice(place * tiles, (place + 1) * tiles)
        totals.append(own_ref[rows, :] + other_ref[rows, :])
    ends = slice(5 * tiles, 5 * tiles + SUBS)
    tails = own_ref[ends, :] + other_ref[ends, :]
    heads = beyond_ref[...] + beyond_other_ref[...]
    corner = jnp.sum(jnp.sum(tails * heads, axis=1, keepdims=True), axis=0, keepdims=True)
    row_at = lax.broadcasted_iota(jnp.int32, (tiles, LANES), 0)
    lane_at = lax.broadcasted_iota(jnp.int32, (tiles, LANES), 1)
    totals[4] = jnp.where((row_at == tiles - 1) & (lane_at == LANES - 1), corner, totals[4])
    for place in range(5):
        for tile in range(tiles):
            densities_ref[place : place + 1, tile * LANES : (tile + 1) * LANES] = totals[place][
                tile : tile + 1, :
            ]
    field_x, field_y, field_z = (exchange_coupling * totals[1 + part] for part in range(3))
    magnet_x, magnet_y, magnet_z = (spin_ref[part] for part in range(3))
    torque = (
        magnet_y * field_z - magnet_z * field_y,
        magnet_z * field_x - magnet_x * field_z,
        magnet_x * field_y - magnet_y * field_x,
    )
    for part, magnet in enumerate((magnet_x, magnet_y, magnet_z)):
        advanced = magnet - spin_ref[3] * torque[part]
        for tile in range(tiles):
            magnet_next_ref[part : part + 1, tile * LANES : (tile + 1) * LANES] = advanced[
                tile : tile + 1, :
            ]

    for copy in copies:
        copy.wait()


def local(
    wave_state,
    potential,
    spin_angle,
    magnet,
    magnetic_mask,
    mode_weight,
    source_amp,
    mode_group,
    energies,
    lead_site,
):
    local_modes, local_sites = wave_state.shape[1:]
    site_count = lax.axis_size("sites")
    mode_count = lax.axis_size("modes")
    assert local_modes == SUBS and local_sites % (LANES * PIECES) == 0
    tiles = local_sites // LANES
    span = float(local_sites * site_count // 8)
    f32 = jnp.float32
    vmem = pl.BlockSpec(memory_space=pltpu.VMEM)
    smem = pl.BlockSpec(memory_space=pltpu.SMEM)
    anywhere = pl.BlockSpec(memory_space=pl.ANY)
    dense = (tiles, LANES)
    payload_rows = 5 * tiles + 2 * SUBS
    kept = lambda array: pltpu.with_memory_space_constraint(array, pltpu.VMEM)

    turned, fields, payload, pack_a, pack_b, source, spin = pl.pallas_call(
        functools.partial(prepare_kernel, local_modes * mode_count),
        out_shape=(
            pltpu.VMEM(wave_state.shape, f32),
            pltpu.VMEM((6,) + dense, f32),
            pltpu.VMEM((payload_rows, LANES), f32),
            pltpu.VMEM((PACK_ROWS, LANES), f32),
            pltpu.VMEM((PACK_ROWS, LANES), f32),
            pltpu.VMEM((17, SUBS, LANES), f32),
            pltpu.VMEM((4,) + dense, f32),
        ),
        in_specs=[anywhere] + [vmem] * 4 + [smem] * 5,
        out_specs=[vmem] * 7,
        scratch_shapes=[
            pltpu.VMEM(wave_state.shape, f32),
            pltpu.SemaphoreType.DMA((PIECES,)),
        ],
        name="prepare",
        cost_estimate=pl.CostEstimate(flops=10_000_000, bytes_accessed=1_500_000, transcendentals=0),
    )(
        wave_state,
        potential.reshape(dense),
        spin_angle.reshape(dense),
        magnet,
        magnetic_mask.reshape(dense),
        mode_weight,
        source_amp,
        mode_group,
        energies,
        lead_site,
    )

    own = payload
    distance = 1
    while 2 * distance < mode_count:
        own = own + lax.ppermute(own, "modes", [(i, i ^ distance) for i in range(mode_count)])
        distance *= 2

    pairs_a = [(i, i + 1) for i in range(0, site_count - 1, 2)]
    pairs_b = [(i, i + 1) for i in range(1, site_count - 1, 2)]
    both = lambda pairs: pairs + [(j, i) for i, j in pairs]
    recv_b = lax.ppermute(pack_b, "sites", both(pairs_b))
    recv_a = lax.ppermute(pack_a, "sites", both(pairs_a))

    other = lax.ppermute(own, "modes", [(i, i ^ distance) for i in range(mode_count)])
    first_sites = slice(5 * tiles + SUBS, payload_rows)
    if mode_count == 4:
        across = [
            (((m if m % 2 == 0 else m ^ 2) * site_count + s + 1), m * site_count + s)
            for m in range(mode_count)
            for s in range(site_count - 1)
        ]
        beyond = lax.ppermute(own[first_sites], ("modes", "sites"), across)
        beyond_other = lax.ppermute(beyond, "modes", [(i, i ^ 1) for i in range(mode_count)])
    else:
        to_left = [(i + 1, i) for i in range(site_count - 1)]
        beyond = lax.ppermute(own[first_sites] + other[first_sites], "sites", to_left)
        beyond_other = jnp.zeros_like(beyond)

    interior, edge = pl.pallas_call(
        functools.partial(interior_kernel, span),
        out_shape=(
            jax.ShapeDtypeStruct(wave_state.shape, f32),
            pltpu.VMEM((8, SUBS, LANES), f32),
        ),
        in_specs=[vmem] * 3,
        out_specs=[anywhere, vmem],
        scratch_shapes=[pltpu.VMEM(wave_state.shape, f32)] * 3
        + [pltpu.SemaphoreType.DMA((PIECES,))],
        name="interior",
        cost_estimate=pl.CostEstimate(flops=20_000_000, bytes_accessed=1_500_000, transcendentals=0),
    )(kept(turned), kept(fields), kept(source))

    next_state, densities, magnet_next = pl.pallas_call(
        functools.partial(finish_kernel, span),
        out_shape=(
            jax.ShapeDtypeStruct(wave_state.shape, f32),
            jax.ShapeDtypeStruct((5, local_sites), f32),
            jax.ShapeDtypeStruct((3, local_sites), f32),
        ),
        in_specs=[anywhere] + [vmem] * 11,
        out_specs=[anywhere, vmem, vmem],
        scratch_shapes=[
            pltpu.VMEM((2, 4, SUBS, LANES), f32),
            pltpu.SemaphoreType.DMA((2,)),
        ],
        input_output_aliases={0: 0},
        name="finish",
        cost_estimate=pl.CostEstimate(flops=1_000_000, bytes_accessed=400_000, transcendentals=0),
    )(
        interior,
        *(
            kept(array)
            for array in (
                edge,
                turned,
                fields,
                recv_a,
                recv_b,
                source,
                own,
                other,
                beyond,
                beyond_other,
                spin,
            )
        ),
    )
    return (next_state, densities, magnet_next)


def solution(mesh):
    return jax.shard_map(
        local,
        mesh=mesh,
        in_specs=(
            P(None, "modes", "sites"),
            P("sites"),
            P("sites"),
            P(None, "sites"),
            P("sites"),
            P("modes"),
            P(None, "modes"),
            P("modes"),
            P(),
            P("modes"),
        ),
        out_specs=(P(None, "modes", "sites"), P(None, "sites"), P(None, "sites")),
        check_vma=False,
    )
```

time: 29.7 us -> 22.2 us (0.75)
  the two profiles are of different devices: /device:TPU:8 before, /device:TPU:3 now
where the time goes in v2:
time: 22.2 us; the launch traced here: 22 us
  starting transfers between devices  9.79 us (44%)
  Pallas kernels  6.31 us (28%)
  waiting for transfers between devices  5.17 us (23%)
  between operations  0.71 us (3%)
    ppermute x1, waiting for transfers between devices, local(): beyond = lax.ppermute(own[first_sites], ('modes', 'sites'), across)  4.22 us
    ppermute x1, starting transfers between devices, local(): recv_b = lax.ppermute(pack_b, 'sites', both(pairs_b))  4.12 us
    pallas_call x1, Pallas kernels, local(): pl.pallas_call(functools.partial(prepare_kernel, local_modes * mode_count...  2.5 us
    pallas_call x1, Pallas kernels, local(): pl.pallas_call(functools.partial(interior_kernel, span), out_shape=(jax.S...  2.13 us
    ppermute x2, starting transfers between devices, local(): lax.ppermute(own, 'modes', [(i, i ^ distance) for i in range(mode_count)])  2.05 us
    ppermute x1, starting transfers between devices, local(): beyond = lax.ppermute(own[first_sites], ('modes', 'sites'), across)  1.92 us
    pallas_call x1, Pallas kernels, local(): pl.pallas_call(functools.partial(finish_kernel, span), out_shape=(jax.Sha...  1.68 us
    ppermute x1, starting transfers between devices, local(): lax.ppermute(beyond, 'modes', [(i, i ^ 1) for i in range(mode_count)])  1.45 us
  transfers between devices with their start and end apart: 6, of which 2 were waited for; matrix products, arithmetic and copies ran while one was open for 0% of the time, Pallas kernels for 10%

profile of v2, /device:TPU:3, one launch (start us, length us, event | category | flops | bytes accessed | tf_op | source)
XLA Modules:
  0.0 22.0 jit_solution(11013838910954582471)
XLA Ops:
  0.6 2.5 %prepare.1 = (f32[4,8,4096]{2,1,0:T(8,128)S(1)}, f32[6,32,128]{2,1,0:T(8,128)S(1)}, f32[176,128]{1,0:T(8,128)S(1)}, f32[40,128]{1,0:T(8,128)S(1)}, f32[40,128]{1...) custom-call(f32[4,8,4096]{2,1,0:T(8,128)} %wave_ref.1, f32[32,128]{1,0:T(8,128)} %bitcast.3, ...), custom_call_target="tpu_custom_call" | custom-call | flops 10000000 | bytes 1500000 | tf_op jit(solution)/shard_map/prepare/pallas_call | solution.py:467
  3.1 0.7 %collective-permute-start.2 = (f32[176,128]{1,0:T(8,128)S(1)}, f32[176,128]{1,0:T(8,128)S(1)}, u32[]{:S(2)}, u32[]{:S(2)}) collective-permute-start(f32[176,128]{1,0:T(8,128)S(1)} %get-tuple-element.19), channel_id=1, source_target_pairs={{0,8},{8,0},{16,24},{24,16},{1,9},{9,1},{17,25},{25,17},{2,10},{10... | collective-permute-start | bytes 270344 | tf_op jit(solution)/shard_map/ppermute | solution.py:502
  3.9 0.9 %collective-permute-done.2 = f32[176,128]{1,0:T(8,128)S(1)} collective-permute-done((f32[176,128]{1,0:T(8,128)S(1)}, f32[176,128]{1,0:T(8,128)S(1)}, u32[]{:S(2)}, u32[]{:S(2)}) %collective-permute-start.2) | collective-permute-done | bytes 90144 | tf_op jit(solution)/shard_map/ppermute | solution.py:502
  4.8 1.3 %collective-permute-start.3 = (f32[176,128]{1,0:T(8,128)S(1)}, f32[176,128]{1,0:T(8,128)S(1)}, u32[]{:S(2)}, u32[]{:S(2)}) collective-permute-start(f32[176,128]{1,0:T(8,128)S(1)} %add.3.refs_7_), channel_id=1, source_target_pairs={{0,16},{8,24},{16,0},{24,8},{1,17},{9,25},{17,1},{25,9},{2,18},{10... | collective-permute-start | bytes 270344 | tf_op jit(solution)/shard_map/ppermute | solution.py:511
  6.1 0.3 %collective-permute-start = (f32[40,128]{1,0:T(8,128)S(1)}, f32[40,128]{1,0:T(8,128)S(1)}, u32[]{:S(2)}, u32[]{:S(2)}) collective-permute-start(f32[40,128]{1,0:T(8,128)S(1)} %get-tuple-element.17), channel_id=1, source_target_pairs={{0,1},{2,3},{4,5},{6,7},{1,0},{3,2},{5,4},{7,6},{8,9},{10,11},{12,... | collective-permute-start | bytes 61448 | tf_op jit(solution)/shard_map/ppermute | solution.py:509
  6.4 4.1 %collective-permute-start.1 = (f32[40,128]{1,0:T(8,128)S(1)}, f32[40,128]{1,0:T(8,128)S(1)}, u32[]{:S(2)}, u32[]{:S(2)}) collective-permute-start(f32[40,128]{1,0:T(8,128)S(1)} %get-tuple-element.18), channel_id=1, source_target_pairs={{1,2},{3,4},{5,6},{2,1},{4,3},{6,5},{9,10},{11,12},{13,14},{10,9},... | collective-permute-start | bytes 61448 | tf_op jit(solution)/shard_map/ppermute | solution.py:508
  10.5 1.9 %collective-permute-start.4 = (f32[8,128]{1,0:T(8,128)S(1)}, f32[8,128]{1,0:T(8,128)S(1)}, u32[]{:S(2)}, u32[]{:S(2)}) collective-permute-start(f32[8,128]{1,0:T(8,128)S(1)} %slice.4), channel_id=1, source_target_pairs={{1,0},{2,1},{3,2},{4,3},{5,4},{6,5},{7,6},{25,8},{26,9},{27,10},{2... | collective-permute-start | bytes 12296 | tf_op jit(solution)/shard_map/ppermute | solution.py:519
  12.5 4.2 %collective-permute-done.4.refs_9_ = f32[8,128]{1,0:T(8,128)S(1)} collective-permute-done((f32[8,128]{1,0:T(8,128)S(1)}, f32[8,128]{1,0:T(8,128)S(1)}, u32[]{:S(2)}, u32[]{:S(2)}) %collective-permute-start.4) | collective-permute-done | bytes 4128 | tf_op jit(solution)/shard_map/ppermute | solution.py:519
  16.7 1.4 %collective-permute-start.5 = (f32[8,128]{1,0:T(8,128)S(1)}, f32[8,128]{1,0:T(8,128)S(1)}, u32[]{:S(2)}, u32[]{:S(2)}) collective-permute-start(f32[8,128]{1,0:T(8,128)S(1)} %collective-permute-done.4.refs_9_), channel_id=1, source_target_pairs={{0,8},{8,0},{16,24},{24,16},{1,9},{9,1},{17,25},{25,17},{2,10},{10... | collective-permute-start | bytes 12296 | tf_op jit(solution)/shard_map/ppermute | solution.py:520
  18.1 2.1 %interior.1 = (f32[4,8,4096]{2,1,0:T(8,128)}, f32[8,8,128]{2,1,0:T(8,128)S(1)}) custom-call(f32[4,8,4096]{2,1,0:T(8,128)S(1)} %get-tuple-element.12.turned_ref.refs_2_, f32[6,32,128]{2,1,0:T(8,128)S(1)} %get-tuple-element.13.fields_ref.refs_3_, f32[17,8,128]{2,1,0:T(8,128)S(1)} %get-tuple-element.14.source_ref.refs_6_), custom_call_target="tpu_custom_call" | custom-call | flops 20000000 | bytes 1500000 | tf_op jit(solution)/shard_map/interior/pallas_call | solution.py:526
  20.3 0.0 collective-permute-done.refs_4_
  20.3 0.0 collective-permute-done.1.refs_5_
  20.3 0.0 collective-permute-done.5.refs_10_
  20.3 0.0 collective-permute-done.3.refs_8_
  20.3 1.7 %finish.1 = (f32[4,8,4096]{2,1,0:T(8,128)}, f32[5,4096]{1,0:T(8,128)}, f32[3,4096]{1,0:T(4,128)}) custom-call(f32[4,8,4096]{2,1,0:T(8,128)} %get-tuple-element.15.refs_0_, f32[8,8,128]{2,1,0:T(8,128)S(1)} %get-tuple-element.16.refs_1_, f32[4,8,4096]{2,1,0:T(8,128)S(1)} %get-tuple-element.12.turned_ref.refs_2_, ...), custom_call_target="tpu_custom_call", output_to_operand_aliasing={{0}: (0, {})} | custom-call | flops 1000000 | bytes 400000 | tf_op jit(solution)/shard_map/finish/pallas_call | solution.py:540
  (2 shorter events, 0.0 us)
Async XLA Ops:
  3.1 1.7 %collective-permute-start.2 = (f32[176,128]{1,0:T(8,128)S(1)}, f32[176,128]{1,0:T(8,128)S(1)}, u32[]{:S(2)}, u32[]{:S(2)}) collective-permute-start(f32[176,128]{1,0:T(8,128)S(1)} %get-tuple-element.19), channel_id=1, source_target_pairs={{0,8},{8,0},{16,24},{24,16},{1,9},{9,1},{17,25},{25,17},{2,10},{10... | collective-permute-start | bytes 270344 | tf_op jit(solution)/shard_map/ppermute | solution.py:502
  4.8 15.5 %collective-permute-start.3 = (f32[176,128]{1,0:T(8,128)S(1)}, f32[176,128]{1,0:T(8,128)S(1)}, u32[]{:S(2)}, u32[]{:S(2)}) collective-permute-start(f32[176,128]{1,0:T(8,128)S(1)} %add.3.refs_7_), channel_id=1, source_target_pairs={{0,16},{8,24},{16,0},{24,8},{1,17},{9,25},{17,1},{25,9},{2,18},{10... | collective-permute-start | bytes 270344 | tf_op jit(solution)/shard_map/ppermute | solution.py:511
  6.1 14.1 %collective-permute-start = (f32[40,128]{1,0:T(8,128)S(1)}, f32[40,128]{1,0:T(8,128)S(1)}, u32[]{:S(2)}, u32[]{:S(2)}) collective-permute-start(f32[40,128]{1,0:T(8,128)S(1)} %get-tuple-element.17), channel_id=1, source_target_pairs={{0,1},{2,3},{4,5},{6,7},{1,0},{3,2},{5,4},{7,6},{8,9},{10,11},{12,... | collective-permute-start | bytes 61448 | tf_op jit(solution)/shard_map/ppermute | solution.py:509
  6.4 13.9 %collective-permute-start.1 = (f32[40,128]{1,0:T(8,128)S(1)}, f32[40,128]{1,0:T(8,128)S(1)}, u32[]{:S(2)}, u32[]{:S(2)}) collective-permute-start(f32[40,128]{1,0:T(8,128)S(1)} %get-tuple-element.18), channel_id=1, source_target_pairs={{1,2},{3,4},{5,6},{2,1},{4,3},{6,5},{9,10},{11,12},{13,14},{10,9},... | collective-permute-start | bytes 61448 | tf_op jit(solution)/shard_map/ppermute | solution.py:508
  10.5 6.1 %collective-permute-start.4 = (f32[8,128]{1,0:T(8,128)S(1)}, f32[8,128]{1,0:T(8,128)S(1)}, u32[]{:S(2)}, u32[]{:S(2)}) collective-permute-start(f32[8,128]{1,0:T(8,128)S(1)} %slice.4), channel_id=1, source_target_pairs={{1,0},{2,1},{3,2},{4,3},{5,4},{6,5},{7,6},{25,8},{26,9},{27,10},{2... | collective-permute-start | bytes 12296 | tf_op jit(solution)/shard_map/ppermute | solution.py:519
  16.7 3.6 %collective-permute-start.5 = (f32[8,128]{1,0:T(8,128)S(1)}, f32[8,128]{1,0:T(8,128)S(1)}, u32[]{:S(2)}, u32[]{:S(2)}) collective-permute-start(f32[8,128]{1,0:T(8,128)S(1)} %collective-permute-done.4.refs_9_), channel_id=1, source_target_pairs={{0,8},{8,0},{16,24},{24,16},{1,9},{9,1},{17,25},{25,17},{2,10},{10... | collective-permute-start | bytes 12296 | tf_op jit(solution)/shard_map/ppermute | solution.py:520

commit v3 on v2

--- a/solution.py
+++ b/solution.py
@@ -15,8 +15,9 @@
 SUBS = 8
 PIECES = 4
 STEP_COEF = (time_step / 4.0, time_step / 3.0, time_step / 2.0, time_step)
-FIELD_ROWS = 8
-PACK_ROWS = 4 * SUBS + FIELD_ROWS
+FIELDS_AT = 4 * SUBS
+HEADS_AT = FIELDS_AT + SUBS
+PACK_ROWS = HEADS_AT + SUBS
 
 
 def lane_iota():
@@ -94,6 +95,8 @@
     payload_ref,
     pack_a_ref,
     pack_b_ref,
+    tails_a_ref,
+    tails_b_ref,
     source_ref,
     spin_ref,
     wave_in,
@@ -227,10 +230,12 @@
         head_column = turned_ref[(part + 2) % 4, :, 0:1]
         head_column = head_column if part < 2 else -head_column
         heads = jnp.where(lanes == slot + part, head_column, heads)
-    payload_ref[5 * tiles : 5 * tiles + SUBS, :] = tails
-    payload_ref[5 * tiles + SUBS : 5 * tiles + 2 * SUBS, :] = heads
-
     even = lax.rem(site_index, 2) == 0
+    last = site_index == lax.axis_size("sites") - 1
+    zero = jnp.zeros((SUBS, LANES), jnp.float32)
+    tails_a_ref[...] = jnp.where(jnp.logical_and(even, jnp.logical_not(last)), tails, zero)
+    tails_b_ref[...] = jnp.where(jnp.logical_or(even, last), zero, tails)
+
     for part in range(4):
         at = slice(part * SUBS, (part + 1) * SUBS)
         head = turned_ref[part, :, 0:LANES]
@@ -238,14 +243,14 @@
         pack_a_ref[at, :] = jnp.where(even, tail, head)
         pack_b_ref[at, :] = jnp.where(even, head, tail)
     for place in range(6):
-        at = slice(32 + place, 33 + place)
+        at = slice(FIELDS_AT + place, FIELDS_AT + place + 1)
         head = fields_ref[place, 0:1, :]
         tail = fields_ref[place, tiles - 1 : tiles, :]
         pack_a_ref[at, :] = jnp.where(even, tail, head)
         pack_b_ref[at, :] = jnp.where(even, head, tail)
-    ends = jnp.where(lax.broadcasted_iota(jnp.int32, (2, LANES), 0) == 0, 1.0, 0.0)
-    pack_a_ref[38:40, :] = ends
-    pack_b_ref[38:40, :] = ends
+    for pack_ref in (pack_a_ref, pack_b_ref):
+        pack_ref[FIELDS_AT + 6 : HEADS_AT, :] = jnp.zeros((2, LANES), jnp.float32)
+        pack_ref[HEADS_AT:PACK_ROWS, :] = heads
 
 
 def region_masks(positions, lead, span, cos_row, sin_row):
@@ -255,12 +260,16 @@
     return jnp.where(inside, cos_row, zero), jnp.where(inside, sin_row, zero)
 
 
-def interior_kernel(span, turned_ref, fields_ref, source_ref, next_ref, edge_ref, *scratch):
+def advance_kernel(
+    span, turned_ref, fields_ref, source_ref, recv_a_ref, recv_b_ref, next_ref, *scratch
+):
     (work_a, work_b, out_ref, sems) = scratch
     tiles = fields_ref.shape[1]
     piece = tiles * LANES // PIECES
     lanes = lane_iota()
-    first_site = lax.axis_index("sites") * (tiles * LANES)
+    site_index = lax.axis_index("sites")
+    even = lax.rem(site_index, 2) == 0
+    first_site = site_index * (tiles * LANES)
     lane_position = (lanes + first_site).astype(jnp.float32)
     lead = source_ref[16]
     zero = (jnp.zeros((SUBS, LANES), jnp.float32),) * 4
@@ -274,144 +283,95 @@
         for part in range(PIECES)
     ]
 
+    inside = {-1: site_index > 0, tiles: site_index < lax.axis_size("sites") - 1}
+    halo = {}
+    for tile, near, far in ((-1, recv_b_ref, recv_a_ref), (tiles, recv_a_ref, recv_b_ref)):
+        base = tuple(
+            jnp.where(
+                inside[tile],
+                jnp.where(
+                    even,
+                    near[part * SUBS : (part + 1) * SUBS, :],
+                    far[part * SUBS : (part + 1) * SUBS, :],
+                ),
+                zero[0],
+            )
+            for part in range(4)
+        )
+        rows = [
+            jnp.where(even, near[place : place + 1, :], far[place : place + 1, :])
+            for place in range(FIELDS_AT, FIELDS_AT + 6)
+        ]
+        halo[tile] = (base, rows)
+    halo_state = {tile: halo[tile][0] for tile in halo}
+
     for step in range(4):
         origin_ref = turned_ref if step == 0 else targets[step - 1]
         target_ref = targets[step]
         parts = [source_ref[step * 4 + part] for part in range(4)]
+        next_halo = {}
 
         def load(tile):
-            if tile == tiles:
+            if tile in halo:
+                return halo_state[tile]
+            if tile > tiles:
                 return zero
             return tuple(
                 origin_ref[part, :, tile * LANES : (tile + 1) * LANES] for part in range(4)
             )
 
         before_up = zero
-        here = load(0)
+        here = load(-1)
         here_up = [shift_from_left(x) for x in here]
         here_down = [shift_from_right(x) for x in here]
-        for tile in range(tiles):
-            at = slice(tile * LANES, (tile + 1) * LANES)
+        for tile in range(-1, tiles + 1):
             after = load(tile + 1)
             after_up = [shift_from_left(x) for x in after]
             after_down = [shift_from_right(x) for x in after]
-            base = tuple(turned_ref[part, :, at] for part in range(4))
-            rows = [fields_ref[place, tile : tile + 1, :] for place in range(6)]
-            hops = [
-                jnp.where(lanes == 0, b, a) + jnp.where(lanes == LANES - 1, d, c)
-                for a, b, c, d in zip(here_up, before_up, here_down, after_down)
-            ]
-            masked = region_masks(
-                lane_position + float(tile * LANES), lead, span, rows[4], rows[5]
-            )
-            out = horner(
-                base, here, hops, rows[:4], source_terms(parts, *masked), STEP_COEF[step]
-            )
-            if step == 3:
-                out = rotate_fore(out, rows[4], rows[5])
-            for part in range(4):
-                target_ref[part, :, at] = out[part]
-            if step == 3 and (tile + 1) * LANES % piece == 0:
-                copies[tile * LANES // piece].start()
+            if tile not in halo or step < 3:
+                if tile in halo:
+                    base, rows = halo[tile]
+                else:
+                    at = slice(tile * LANES, (tile + 1) * LANES)
+                    base = tuple(turned_ref[part, :, at] for part in range(4))
+                    rows = [fields_ref[place, tile : tile + 1, :] for place in range(6)]
+                hops = [
+                    jnp.where(lanes == 0, b, a) + jnp.where(lanes == LANES - 1, d, c)
+                    for a, b, c, d in zip(here_up, before_up, here_down, after_down)
+                ]
+                masked = region_masks(
+                    lane_position + float(tile * LANES), lead, span, rows[4], rows[5]
+                )
+                out = horner(
+                    base, here, hops, rows[:4], source_terms(parts, *masked), STEP_COEF[step]
+                )
+                if tile in halo:
+                    next_halo[tile] = tuple(jnp.where(inside[tile], x, zero[0]) for x in out)
+                else:
+                    if step == 3:
+                        out = rotate_fore(out, rows[4], rows[5])
+                    for part in range(4):
+                        target_ref[part, :, at] = out[part]
+                    if step == 3 and (tile + 1) * LANES % piece == 0:
+                        copies[tile * LANES // piece].start()
             before_up, here, here_up, here_down = here_up, after, after_up, after_down
-
-    final = (tiles - 1) * LANES
-    for part in range(4):
-        edge_ref[part] = out_ref[part, :, 0:LANES]
-        edge_ref[4 + part] = out_ref[part, :, final : final + LANES]
+        halo_state = next_halo
+
     for copy in copies:
         copy.wait()
 
 
-def finish_kernel(span, *refs):
-    (
-        interior_ref,
-        edge_ref,
-        turned_ref,
-        fields_ref,
-        recv_a_ref,
-        recv_b_ref,
-        source_ref,
-        own_ref,
-        other_ref,
-        beyond_ref,
-        beyond_other_ref,
-        spin_ref,
-        next_ref,
-        densities_ref,
-        magnet_next_ref,
-        patch_ref,
-        sems,
-    ) = refs
-    tiles = fields_ref.shape[1]
-    lanes = lane_iota()
-    first_site = lax.axis_index("sites") * (tiles * LANES)
-    even = lax.rem(lax.axis_index("sites"), 2) == 0
-    lead = source_ref[16]
-    final = (tiles - 1) * LANES
-    half = LANES // 2
-    upper = lanes >= half
-    upper_row = upper[0:1, :]
-
-    for side in range(2):
-        near, far = (recv_b_ref, recv_a_ref) if side == 0 else (recv_a_ref, recv_b_ref)
-
-        def joined(pack_at, own, upper_half):
-            fetched = jnp.where(even, near[pack_at, :], far[pack_at, :])
-            if side == 0:
-                return jnp.where(upper_half, fetched, own)
-            return jnp.where(upper_half, own, fetched)
-
-        edge_tile = 0 if side == 0 else tiles - 1
-        at = slice(edge_tile * LANES, (edge_tile + 1) * LANES)
-        base = tuple(
-            joined(slice(part * SUBS, (part + 1) * SUBS), turned_ref[part, :, at], upper)
-            for part in range(4)
-        )
-        rows = [
-            joined(
-                slice(32 + place, 33 + place),
-                fields_ref[place, edge_tile : edge_tile + 1, :],
-                upper_row,
-            )
-            for place in range(6)
-        ]
-        inside = joined(slice(38, 39), jnp.ones((1, LANES), jnp.float32), upper_row)
-        if side == 0:
-            position = first_site + jnp.where(upper, lanes - LANES, lanes)
-        else:
-            position = first_site + final + jnp.where(upper, lanes, lanes + LANES)
-        masked = region_masks(position.astype(jnp.float32), lead, span, rows[4], rows[5])
-        state = base
-        for step in range(4):
-            parts = [source_ref[step * 4 + part] for part in range(4)]
-            hops = [shift_from_left(x) + shift_from_right(x) for x in state]
-            state = horner(base, state, hops, rows[:4], source_terms(parts, *masked), STEP_COEF[step])
-            if step < 3:
-                state = tuple(inside * x for x in state)
-        out = rotate_fore(state, rows[4], rows[5])
-        fresh = lanes < 4 if side == 0 else lanes >= LANES - 4
-        for part in range(4):
-            patch_ref[side, part] = jnp.where(fresh, out[part], edge_ref[side * 4 + part])
-    copies = [
-        pltpu.make_async_copy(
-            patch_ref.at[side],
-            next_ref.at[:, :, pl.ds(side * final, LANES)],
-            sems.at[side],
-        )
-        for side in range(2)
-    ]
-    for copy in copies:
-        copy.start()
-
+def finish_kernel(
+    own_ref, other_ref, corner_a_ref, corner_b_ref, spin_ref, densities_ref, magnet_next_ref
+):
+    tiles = spin_ref.shape[1]
     totals = []
     for place in range(5):
         rows = slice(place * tiles, (place + 1) * tiles)
         totals.append(own_ref[rows, :] + other_ref[rows, :])
     ends = slice(5 * tiles, 5 * tiles + SUBS)
-    tails = own_ref[ends, :] + other_ref[ends, :]
-    heads = beyond_ref[...] + beyond_other_ref[...]
-    corner = jnp.sum(jnp.sum(tails * heads, axis=1, keepdims=True), axis=0, keepdims=True)
+    products = (own_ref[ends, :] + other_ref[ends, :]) + (corner_a_ref[...] + corner_b_ref[...])
+    corner = jnp.sum(jnp.sum(products, axis=1, keepdims=True), axis=0, keepdims=True)
     row_at = lax.broadcasted_iota(jnp.int32, (tiles, LANES), 0)
     lane_at = lax.broadcasted_iota(jnp.int32, (tiles, LANES), 1)
     totals[4] = jnp.where((row_at == tiles - 1) & (lane_at == LANES - 1), corner, totals[4])
@@ -433,9 +393,6 @@
             magnet_next_ref[part : part + 1, tile * LANES : (tile + 1) * LANES] = advanced[
                 tile : tile + 1, :
             ]
-
-    for copy in copies:
-        copy.wait()
 
 
 def local(
@@ -461,22 +418,23 @@
     smem = pl.BlockSpec(memory_space=pltpu.SMEM)
     anywhere = pl.BlockSpec(memory_space=pl.ANY)
     dense = (tiles, LANES)
-    payload_rows = 5 * tiles + 2 * SUBS
     kept = lambda array: pltpu.with_memory_space_constraint(array, pltpu.VMEM)
 
-    turned, fields, payload, pack_a, pack_b, source, spin = pl.pallas_call(
+    turned, fields, payload, pack_a, pack_b, tails_a, tails_b, source, spin = pl.pallas_call(
         functools.partial(prepare_kernel, local_modes * mode_count),
         out_shape=(
             pltpu.VMEM(wave_state.shape, f32),
             pltpu.VMEM((6,) + dense, f32),
-            pltpu.VMEM((payload_rows, LANES), f32),
+            pltpu.VMEM((5 * tiles, LANES), f32),
             pltpu.VMEM((PACK_ROWS, LANES), f32),
             pltpu.VMEM((PACK_ROWS, LANES), f32),
+            pltpu.VMEM((SUBS, LANES), f32),
+            pltpu.VMEM((SUBS, LANES), f32),
             pltpu.VMEM((17, SUBS, LANES), f32),
             pltpu.VMEM((4,) + dense, f32),
         ),
         in_specs=[anywhere] + [vmem] * 4 + [smem] * 5,
-        out_specs=[vmem] * 7,
+        out_specs=[vmem] * 9,
         scratch_shapes=[
             pltpu.VMEM(wave_state.shape, f32),
             pltpu.SemaphoreType.DMA((PIECES,)),
@@ -496,82 +454,62 @@
         lead_site,
     )
 
-    own = payload
-    distance = 1
-    while 2 * distance < mode_count:
-        own = own + lax.ppermute(own, "modes", [(i, i ^ distance) for i in range(mode_count)])
-        distance *= 2
-
-    pairs_a = [(i, i + 1) for i in range(0, site_count - 1, 2)]
-    pairs_b = [(i, i + 1) for i in range(1, site_count - 1, 2)]
-    both = lambda pairs: pairs + [(j, i) for i, j in pairs]
-    recv_b = lax.ppermute(pack_b, "sites", both(pairs_b))
-    recv_a = lax.ppermute(pack_a, "sites", both(pairs_a))
-
-    other = lax.ppermute(own, "modes", [(i, i ^ distance) for i in range(mode_count)])
-    first_sites = slice(5 * tiles + SUBS, payload_rows)
+    def swap_sites(pack, pairs):
+        partner = {i: j for pair in pairs for i, j in (pair, pair[::-1])}
+        whole = [
+            (
+                m * site_count + s,
+                m * site_count + partner[s] if s in partner else (m ^ 1) * site_count + s,
+            )
+            for m in range(mode_count)
+            for s in range(site_count)
+        ]
+        return lax.ppermute(pack, ("modes", "sites"), whole)
+
+    def swap_modes(array, distance):
+        return lax.ppermute(array, "modes", [(i, i ^ distance) for i in range(mode_count)])
+
+    recv_b = swap_sites(pack_b, [(i, i + 1) for i in range(1, site_count - 1, 2)])
+    recv_a = swap_sites(pack_a, [(i, i + 1) for i in range(0, site_count - 1, 2)])
+    product = tails_a * recv_a[HEADS_AT:] + tails_b * recv_b[HEADS_AT:]
+
     if mode_count == 4:
-        across = [
-            (((m if m % 2 == 0 else m ^ 2) * site_count + s + 1), m * site_count + s)
-            for m in range(mode_count)
-            for s in range(site_count - 1)
-        ]
-        beyond = lax.ppermute(own[first_sites], ("modes", "sites"), across)
-        beyond_other = lax.ppermute(beyond, "modes", [(i, i ^ 1) for i in range(mode_count)])
+        own = payload + swap_modes(payload, 1)
+        own = jnp.concatenate([own, product])
+        other = swap_modes(own, 2)
+        corner_a = swap_modes(product, 3)
+        corner_b = swap_modes(product, 1)
     else:
-        to_left = [(i + 1, i) for i in range(site_count - 1)]
-        beyond = lax.ppermute(own[first_sites] + other[first_sites], "sites", to_left)
-        beyond_other = jnp.zeros_like(beyond)
-
-    interior, edge = pl.pallas_call(
-        functools.partial(interior_kernel, span),
-        out_shape=(
-            jax.ShapeDtypeStruct(wave_state.shape, f32),
-            pltpu.VMEM((8, SUBS, LANES), f32),
-        ),
-        in_specs=[vmem] * 3,
-        out_specs=[anywhere, vmem],
+        own = jnp.concatenate([payload, product])
+        distance = 1
+        while 2 * distance < mode_count:
+            own = own + swap_modes(own, distance)
+            distance *= 2
+        other = swap_modes(own, distance)
+        corner_a = corner_b = jnp.zeros_like(product)
+
+    next_state = pl.pallas_call(
+        functools.partial(advance_kernel, span),
+        out_shape=jax.ShapeDtypeStruct(wave_state.shape, f32),
+        in_specs=[vmem] * 5,
+        out_specs=anywhere,
         scratch_shapes=[pltpu.VMEM(wave_state.shape, f32)] * 3
         + [pltpu.SemaphoreType.DMA((PIECES,))],
-        name="interior",
+        name="advance",
         cost_estimate=pl.CostEstimate(flops=20_000_000, bytes_accessed=1_500_000, transcendentals=0),
-    )(kept(turned), kept(fields), kept(source))
-
-    next_state, densities, magnet_next = pl.pallas_call(
-        functools.partial(finish_kernel, span),
+    )(kept(turned), kept(fields), kept(source), kept(recv_a), kept(recv_b))
+
+    densities, magnet_next = pl.pallas_call(
+        finish_kernel,
         out_shape=(
-            jax.ShapeDtypeStruct(wave_state.shape, f32),
             jax.ShapeDtypeStruct((5, local_sites), f32),
             jax.ShapeDtypeStruct((3, local_sites), f32),
         ),
-        in_specs=[anywhere] + [vmem] * 11,
-        out_specs=[anywhere, vmem, vmem],
-        scratch_shapes=[
-            pltpu.VMEM((2, 4, SUBS, LANES), f32),
-            pltpu.SemaphoreType.DMA((2,)),
-        ],
-        input_output_aliases={0: 0},
+        in_specs=[vmem] * 5,
+        out_specs=[vmem, vmem],
         name="finish",
         cost_estimate=pl.CostEstimate(flops=1_000_000, bytes_accessed=400_000, transcendentals=0),
-    )(
-        interior,
-        *(
-            kept(array)
-            for array in (
-                edge,
-                turned,
-                fields,
-                recv_a,
-                recv_b,
-                source,
-                own,
-                other,
-                beyond,
-                beyond_other,
-                spin,
-            )
-        ),
-    )
+    )(kept(own), kept(other), kept(corner_a), kept(corner_b), kept(spin))
     return (next_state, densities, magnet_next)
 
 

time: 22.2 us -> 15.7 us (0.71)
  the two profiles are of different devices: /device:TPU:3 before, /device:TPU:9 now
where the time goes in v3:
time: 15.7 us; the launch traced here: 15.5 us
  starting transfers between devices  6.04 us (38%)
  Pallas kernels  5.37 us (34%)
  waiting for transfers between devices  3.4 us (22%)
  between operations  0.67 us (4%)
    ppermute x4, starting transfers between devices, swap_modes(): lax.ppermute(array, 'modes', [(i, i ^ distance) for i in range(mode_count)])  4.76 us
    ppermute x2, waiting for transfers between devices, swap_sites(): return lax.ppermute(pack, ('modes', 'sites'), whole)  2.62 us
    pallas_call x1, Pallas kernels, local(): pl.pallas_call(functools.partial(prepare_kernel, local_modes * mode_count...  2.49 us
    pallas_call x1, Pallas kernels, local(): pl.pallas_call(functools.partial(advance_kernel, span), out_shape=jax.Sha...  2.12 us
    ppermute x2, starting transfers between devices, swap_sites(): return lax.ppermute(pack, ('modes', 'sites'), whole)  1.28 us
    ppermute x4, waiting for transfers between devices, swap_modes(): lax.ppermute(array, 'modes', [(i, i ^ distance) for i in range(mode_count)])  0.78 us
    pallas_call x1, Pallas kernels, local(): pl.pallas_call(finish_kernel, out_shape=(jax.ShapeDtypeStruct((5, local_s...  0.76 us
  transfers between devices with their start and end apart: 6, of which 3 were waited for; matrix products, arithmetic and copies ran while one was open for 0% of the time, Pallas kernels for 14%

profile of v3, /device:TPU:9, one launch (start us, length us, event | category | flops | bytes accessed | tf_op | source)
XLA Modules:
  0.0 15.5 jit_solution(16167175550500136612)
XLA Ops:
  0.6 2.5 %prepare.1 = (f32[4,8,4096]{2,1,0:T(8,128)S(1)}, f32[6,32,128]{2,1,0:T(8,128)S(1)}, f32[160,128]{1,0:T(8,128)S(1)}, f32[48,128]{1,0:T(8,128)S(1)}, f32[48,128]{1...) custom-call(f32[4,8,4096]{2,1,0:T(8,128)} %wave_ref.1, ...), custom_call_target="tpu_custom_call" | custom-call | flops 10000000 | bytes 1500000 | tf_op jit(solution)/shard_map/prepare/pallas_call | solution.py:423
  3.1 1.3 %collective-permute-start = (f32[48,128]{1,0:T(8,128)S(1)}, f32[48,128]{1,0:T(8,128)S(1)}, u32[]{:S(2)}, u32[]{:S(2)}) collective-permute-start(f32[48,128]{1,0:T(8,128)S(1)} %get-tuple-element.17), channel_id=1, source_target_pairs={{0,1},{1,0},{2,3},{3,2},{4,5},{5,4},{6,7},{7,6},{8,9},{9,8},{10,11... | collective-permute-start | bytes 73736 | tf_op jit(solution)/shard_map/ppermute | solution.py:467
  4.4 0.0 collective-permute-start.1
  4.4 1.0 %collective-permute-start.2 = (f32[160,128]{1,0:T(8,128)S(1)}, f32[160,128]{1,0:T(8,128)S(1)}, u32[]{:S(2)}, u32[]{:S(2)}) collective-permute-start(f32[160,128]{1,0:T(8,128)S(1)} %get-tuple-element.19), channel_id=1, source_target_pairs={{0,8},{8,0},{16,24},{24,16},{1,9},{9,1},{17,25},{25,17},{2,10},{10... | collective-permute-start | bytes 245768 | tf_op jit(solution)/shard_map/ppermute | solution.py:470
  5.4 0.5 %collective-permute-done.recv_a_ref = f32[48,128]{1,0:T(8,128)S(1)} collective-permute-done((f32[48,128]{1,0:T(8,128)S(1)}, f32[48,128]{1,0:T(8,128)S(1)}, u32[]{:S(2)}, u32[]{:S(2)}) %collective-permute-start) | collective-permute-done | bytes 24608 | tf_op jit(solution)/shard_map/ppermute | solution.py:467
  5.9 2.1 %collective-permute-done.1.recv_b_ref = f32[48,128]{1,0:T(8,128)S(1)} collective-permute-done((f32[48,128]{1,0:T(8,128)S(1)}, f32[48,128]{1,0:T(8,128)S(1)}, u32[]{:S(2)}, u32[]{:S(2)}) %collective-permute-start.1) | collective-permute-done | bytes 24608 | tf_op jit(solution)/shard_map/ppermute | solution.py:467
  8.0 0.0 collective-permute-done.2
  8.0 1.3 %collective-permute-start.3 = (f32[168,128]{1,0:T(8,128)S(1)}, f32[168,128]{1,0:T(8,128)S(1)}, u32[]{:S(2)}, u32[]{:S(2)}) collective-permute-start(f32[168,128]{1,0:T(8,128)S(1)} %pad_maximum_fusion.own_ref), channel_id=1, source_target_pairs={{0,16},{8,24},{16,0},{24,8},{1,17},{9,25},{17,1},{25,9},{2,18},{10... | collective-permute-start | bytes 258056 | tf_op jit(solution)/shard_map/ppermute | solution.py:470
  9.3 2.4 %collective-permute-start.5 = (f32[8,128]{1,0:T(8,128)S(1)}, f32[8,128]{1,0:T(8,128)S(1)}, u32[]{:S(2)}, u32[]{:S(2)}) collective-permute-start(f32[8,128]{1,0:T(8,128)S(1)} %fusion), channel_id=1, source_target_pairs={{0,8},{8,0},{16,24},{24,16},{1,9},{9,1},{17,25},{25,17},{2,10},{10... | collective-permute-start | bytes 12296 | tf_op jit(solution)/shard_map/ppermute | solution.py:470
  11.7 0.1 collective-permute-start.4
  11.8 2.1 %advance.1 = f32[4,8,4096]{2,1,0:T(8,128)} custom-call(f32[4,8,4096]{2,1,0:T(8,128)S(1)} %get-tuple-element.14.turned_ref, f32[6,32,128]{2,1,0:T(8,128)S(1)} %get-tuple-element.15.fields_ref, f32[17,8,128]{2,1,0:T(8,128)S(1)} %get-tuple-element.16.source_ref, f32[48,128]{1,0:T(8,128)S(1)} %collective-permute-done.recv_a_ref, ...), custom_call_target="tpu_custom_call" | custom-call | flops 20000000 | bytes 1500000 | tf_op jit(solution)/shard_map/advance/pallas_call | solution.py:491
  14.0 0.0 collective-permute-done.5.corner_b_ref
  14.0 0.8 %collective-permute-done.4.corner_a_ref = f32[8,128]{1,0:T(8,128)S(1)} collective-permute-done((f32[8,128]{1,0:T(8,128)S(1)}, f32[8,128]{1,0:T(8,128)S(1)}, u32[]{:S(2)}, u32[]{:S(2)}) %collective-permute-start.4) | collective-permute-done | bytes 4128 | tf_op jit(solution)/shard_map/ppermute | solution.py:470
  14.7 0.0 collective-permute-done.3.other_ref
  14.7 0.8 %finish.1 = (f32[5,4096]{1,0:T(8,128)}, f32[3,4096]{1,0:T(4,128)}) custom-call(f32[168,128]{1,0:T(8,128)S(1)} %pad_maximum_fusion.own_ref, f32[168,128]{1,0:T(8,128)S(1)} %collective-permute-done.3.other_ref, f32[8,128]{1,0:T(8,128)S(1)} %collective-permute-done.4.corner_a_ref, f32[8,128]{1,0:T(8,128)S(1)} %collective-permute-done.5.corner_b_ref, ...), custom_call_target="tpu_custom_call" | custom-call | flops 1000000 | bytes 400000 | tf_op jit(solution)/shard_map/finish/pallas_call | solution.py:502
  (3 shorter events, 0.0 us)
Async XLA Ops:
  3.1 2.7 %collective-permute-start = (f32[48,128]{1,0:T(8,128)S(1)}, f32[48,128]{1,0:T(8,128)S(1)}, u32[]{:S(2)}, u32[]{:S(2)}) collective-permute-start(f32[48,128]{1,0:T(8,128)S(1)} %get-tuple-element.17), channel_id=1, source_target_pairs={{0,1},{1,0},{2,3},{3,2},{4,5},{5,4},{6,7},{7,6},{8,9},{9,8},{10,11... | collective-permute-start | bytes 73736 | tf_op jit(solution)/shard_map/ppermute | solution.py:467
  4.4 3.6 %collective-permute-start.1 = (f32[48,128]{1,0:T(8,128)S(1)}, f32[48,128]{1,0:T(8,128)S(1)}, u32[]{:S(2)}, u32[]{:S(2)}) collective-permute-start(f32[48,128]{1,0:T(8,128)S(1)} %get-tuple-element.18), channel_id=1, source_target_pairs={{0,8},{1,2},{2,1},{3,4},{4,3},{5,6},{6,5},{7,15},{8,0},{9,10},{10,... | collective-permute-start | bytes 73736 | tf_op jit(solution)/shard_map/ppermute | solution.py:467
  4.4 3.6 %collective-permute-start.2 = (f32[160,128]{1,0:T(8,128)S(1)}, f32[160,128]{1,0:T(8,128)S(1)}, u32[]{:S(2)}, u32[]{:S(2)}) collective-permute-start(f32[160,128]{1,0:T(8,128)S(1)} %get-tuple-element.19), channel_id=1, source_target_pairs={{0,8},{8,0},{16,24},{24,16},{1,9},{9,1},{17,25},{25,17},{2,10},{10... | collective-permute-start | bytes 245768 | tf_op jit(solution)/shard_map/ppermute | solution.py:470
  8.0 6.7 %collective-permute-start.3 = (f32[168,128]{1,0:T(8,128)S(1)}, f32[168,128]{1,0:T(8,128)S(1)}, u32[]{:S(2)}, u32[]{:S(2)}) collective-permute-start(f32[168,128]{1,0:T(8,128)S(1)} %pad_maximum_fusion.own_ref), channel_id=1, source_target_pairs={{0,16},{8,24},{16,0},{24,8},{1,17},{9,25},{17,1},{25,9},{2,18},{10... | collective-permute-start | bytes 258056 | tf_op jit(solution)/shard_map/ppermute | solution.py:470
  9.3 4.6 %collective-permute-start.5 = (f32[8,128]{1,0:T(8,128)S(1)}, f32[8,128]{1,0:T(8,128)S(1)}, u32[]{:S(2)}, u32[]{:S(2)}) collective-permute-start(f32[8,128]{1,0:T(8,128)S(1)} %fusion), channel_id=1, source_target_pairs={{0,8},{8,0},{16,24},{24,16},{1,9},{9,1},{17,25},{25,17},{2,10},{10... | collective-permute-start | bytes 12296 | tf_op jit(solution)/shard_map/ppermute | solution.py:470
  11.7 3.0 %collective-permute-start.4 = (f32[8,128]{1,0:T(8,128)S(1)}, f32[8,128]{1,0:T(8,128)S(1)}, u32[]{:S(2)}, u32[]{:S(2)}) collective-permute-start(f32[8,128]{1,0:T(8,128)S(1)} %fusion), channel_id=1, source_target_pairs={{0,24},{8,16},{16,8},{24,0},{1,25},{9,17},{17,9},{25,1},{2,26},{10... | collective-permute-start | bytes 12296 | tf_op jit(solution)/shard_map/ppermute | solution.py:470

commit v4 on v3

v4 whole, which is shorter than its diff:
```python
import functools
import math

import jax
import jax.numpy as jnp
from jax import lax
from jax.experimental import pallas as pl
from jax.experimental.pallas import tpu as pltpu
from jax.sharding import PartitionSpec as P

time_step = 0.6
start_time = 10.0
exchange_coupling = 0.5
LANES = 128
SUBS = 8
PIECES = 4
STEP_COEF = (time_step / 4.0, time_step / 3.0, time_step / 2.0, time_step)
REACH = 4


def lane_iota():
    return lax.broadcasted_iota(jnp.int32, (SUBS, LANES), 1)


def sub_iota():
    return lax.broadcasted_iota(jnp.int32, (SUBS, LANES), 0)


def shift_from_left(tile):
    return pltpu.roll(tile, 1, 1)


def shift_from_right(tile):
    return pltpu.roll(tile, LANES - 1, 1)


def column(row):
    count = row.shape[1]
    shape = (count, count)
    same = lax.broadcasted_iota(jnp.int32, shape, 0) == lax.broadcasted_iota(jnp.int32, shape, 1)
    spread = jnp.broadcast_to(row, shape)
    return jnp.sum(jnp.where(same, spread, jnp.zeros_like(spread)), axis=1, keepdims=True)


def source_terms(parts, masked_cos, masked_sin):
    up_real, down_real, up_imag, down_imag = parts
    return (
        masked_cos * up_real + masked_sin * down_real,
        masked_cos * down_real - masked_sin * up_real,
        masked_cos * up_imag + masked_sin * down_imag,
        masked_cos * down_imag - masked_sin * up_imag,
    )


def rotate_fore(state, cos_row, sin_row):
    return (
        cos_row * state[0] - sin_row * state[1],
        sin_row * state[0] + cos_row * state[1],
        cos_row * state[2] - sin_row * state[3],
        sin_row * state[2] + cos_row * state[3],
    )


def rotate_back(state, cos_row, sin_row):
    return (
        cos_row * state[0] + sin_row * state[1],
        cos_row * state[1] - sin_row * state[0],
        cos_row * state[2] + sin_row * state[3],
        cos_row * state[3] - sin_row * state[2],
    )


def horner(base, state, hops, fields, source, coef):
    up_real, down_real, up_imag, down_imag = state
    plus, minus, field_x, field_y = fields
    h_up_real = plus * up_real + field_x * down_real + field_y * down_imag - hops[0] + source[0]
    h_down_real = minus * down_real + field_x * up_real - field_y * up_imag - hops[1] + source[1]
    h_up_imag = plus * up_imag + field_x * down_imag - field_y * down_real - hops[2] + source[2]
    h_down_imag = minus * down_imag + field_x * up_imag + field_y * up_real - hops[3] + source[3]
    return (
        base[0] + coef * h_up_imag,
        base[1] + coef * h_down_imag,
        base[2] - coef * h_up_real,
        base[3] - coef * h_down_real,
    )


def field_rows(potential, cosine, sine, field):
    field_x, field_y, field_z = field
    cos_two = cosine * cosine - sine * sine
    sin_two = 2.0 * (cosine * sine)
    turned_z = field_z * cos_two + field_x * sin_two
    return (
        potential + turned_z,
        potential - turned_z,
        field_x * cos_two - field_z * sin_two,
        field_y,
    )


def edge_kernel(
    wave_ref,
    potential_ref,
    angle_ref,
    magnet_ref,
    mask_ref,
    weight_ref,
    amp_ref,
    group_ref,
    energies_ref,
    lead_ref,
    pack_a_ref,
    pack_b_ref,
    tails_a_ref,
    tails_b_ref,
    weight_out_ref,
    potential_in,
    magnet_in,
    mask_in,
    amp_in,
    group_in,
    energies_in,
    lead_in,
    angle_in,
    edge_in,
    weight_in,
    sems,
):
    tiles = angle_ref.shape[0]
    final = (tiles - 1) * LANES
    moves = [
        (wave_ref.at[:, :, pl.ds(side * final, LANES)], edge_in.at[side]) for side in range(2)
    ]
    moves += [
        (angle_ref, angle_in),
        (mask_ref, mask_in),
        (magnet_ref, magnet_in),
        (potential_ref, potential_in),
    ]
    moves += [(weight_ref, weight_in)]
    moves += [
        (amp_ref, amp_in),
        (group_ref, group_in),
        (energies_ref, energies_in),
        (lead_ref, lead_in),
    ]
    moving = [
        pltpu.make_async_copy(source, target, sems.at[place])
        for place, (source, target) in enumerate(moves)
    ]
    for copy in moving:
        copy.start()
    lanes = lane_iota()
    site_index = lax.axis_index("sites")
    even = lax.rem(site_index, 2) == 0
    last = site_index == lax.axis_size("sites") - 1
    zero = jnp.zeros((SUBS, LANES), jnp.float32)
    for copy in moving[:7]:
        copy.wait()
    weight = jnp.broadcast_to(column(weight_in[...]), (SUBS, LANES))
    weight_out_ref[...] = weight

    turned = []
    fields = []
    for side, row in ((0, 0), (1, tiles - 1)):
        at = slice(row * LANES, (row + 1) * LANES)
        cosine = jnp.cos(angle_in[row : row + 1, :])
        sine = jnp.sin(angle_in[row : row + 1, :])
        strength = exchange_coupling * mask_in[row : row + 1, :].astype(jnp.float32)
        field = [strength * magnet_in[part : part + 1, at] for part in range(3)]
        potential = potential_in[row : row + 1, :]
        fields.append(field_rows(potential, cosine, sine, field) + (cosine, sine))
        turned.append(rotate_back([edge_in[side, part] for part in range(4)], cosine, sine))
    head, tail = turned

    tails = zero
    for part in range(4):
        end = tail[(part + 2) % 4][:, LANES - 1 : LANES]
        tails = jnp.where(lanes == REACH * part, -end if part < 2 else end, tails)
    tails_a_ref[...] = jnp.where(jnp.logical_and(even, jnp.logical_not(last)), tails, zero)
    tails_b_ref[...] = jnp.where(jnp.logical_or(even, last), zero, tails)

    rows = sub_iota()
    packs = []
    for side in range(2):
        blocks = list(turned[side])
        block = jnp.broadcast_to(fields[side][0], (SUBS, LANES))
        for place in range(1, 6):
            block = jnp.where(rows == place, fields[side][place], block)
        blocks.append(block)
        pack = zero
        for part, block in enumerate(blocks):
            shift = REACH * (part + side) % LANES
            moved = pltpu.roll(block, shift, 1) if shift else block
            pack = jnp.where(lanes // REACH == part, moved, pack)
        packs.append(pack)
    pack_a_ref[...] = jnp.where(even, packs[1], packs[0])
    pack_b_ref[...] = jnp.where(even, packs[0], packs[1])

    for copy in moving[7:]:
        copy.wait()


def density_kernel(all_modes, wave_ref, angle_ref, weight_ref, turned_ref, trig_ref, payload_ref):
    tiles = angle_ref.shape[0]
    lanes = lane_iota()
    trig_ref[0] = jnp.cos(angle_ref[...])
    trig_ref[1] = jnp.sin(angle_ref[...])

    weight = weight_ref[...]
    charge_scale = 1.0 / all_modes
    spin_scale = 1.0 / math.sqrt(all_modes)
    nothing = (jnp.zeros((SUBS, LANES), jnp.float32),) * 4

    def rotated(tile):
        if tile == tiles:
            return nothing
        at = slice(tile * LANES, (tile + 1) * LANES)
        cos_row = trig_ref[0, tile : tile + 1, :]
        sin_row = trig_ref[1, tile : tile + 1, :]
        out = rotate_back([wave_ref[part, :, at] for part in range(4)], cos_row, sin_row)
        for part in range(4):
            turned_ref[part, :, at] = out[part]
        return out

    here = rotated(0)
    here_rolled = [shift_from_right(x) for x in here]
    for tile in range(tiles):
        at = slice(tile * LANES, (tile + 1) * LANES)
        after = rotated(tile + 1)
        after_rolled = [shift_from_right(x) for x in after]
        up_real, down_real, up_imag, down_imag = (wave_ref[part, :, at] for part in range(4))
        follow = [jnp.where(lanes == LANES - 1, b, a) for a, b in zip(here_rolled, after_rolled)]
        up_square = up_real * up_real + up_imag * up_imag
        down_square = down_real * down_real + down_imag * down_imag
        current = (
            here[0] * follow[2] + here[1] * follow[3] - here[2] * follow[0] - here[3] * follow[1]
        )
        rows = (
            (up_square + down_square, charge_scale),
            (up_real * down_real + up_imag * down_imag, 2.0 * spin_scale),
            (up_real * down_imag - up_imag * down_real, 2.0 * spin_scale),
            (up_square - down_square, spin_scale),
            (current, 2.0 * spin_scale),
        )
        for place, (value, scale) in enumerate(rows):
            payload_ref[place * tiles + tile : place * tiles + tile + 1, :] = scale * jnp.sum(
                value * weight, axis=0, keepdims=True
            )
        here, here_rolled = after, after_rolled


def region_masks(positions, lead, span, cos_row, sin_row):
    offset = positions - lead
    inside = (offset >= 0.0) & (offset < span)
    zero = jnp.zeros((SUBS, LANES), jnp.float32)
    return jnp.where(inside, cos_row, zero), jnp.where(inside, sin_row, zero)


def setup_kernel(
    scale,
    weight_ref,
    trig_ref,
    potential_ref,
    magnet_ref,
    mask_ref,
    amp_ref,
    group_ref,
    energies_ref,
    lead_ref,
    fields_ref,
    source_ref,
    spin_ref,
    scaled_ref,
):
    tiles = trig_ref.shape[1]
    scaled_ref[...] = scale * weight_ref[...]
    cosine = trig_ref[0]
    sine = trig_ref[1]
    for part in range(3):
        for tile in range(tiles):
            spin_ref[part, tile : tile + 1, :] = magnet_ref[
                part : part + 1, tile * LANES : (tile + 1) * LANES
            ]
    mask = mask_ref[...].astype(jnp.float32)
    strength = exchange_coupling * mask
    field = [strength * spin_ref[part] for part in range(3)]
    for place, value in enumerate(field_rows(potential_ref[...], cosine, sine, field)):
        fields_ref[place] = value
    spin_ref[3] = time_step * mask

    table = (SUBS, energies_ref.shape[1])
    chosen = column(group_ref[...].astype(jnp.float32)) == lax.broadcasted_iota(
        jnp.int32, table, 1
    ).astype(jnp.float32)
    values = jnp.broadcast_to(energies_ref[...], table)
    energy = jnp.sum(jnp.where(chosen, values, jnp.zeros_like(values)), axis=1, keepdims=True)
    energy = jnp.broadcast_to(energy, (SUBS, LANES))
    amps = [
        jnp.broadcast_to(column(amp_ref[part : part + 1, :]), (SUBS, LANES)) for part in range(4)
    ]
    stages = []
    for offset in (0.0, 0.5 * time_step, time_step):
        phase = energy * (start_time + offset)
        cos_phase = jnp.cos(phase)
        sin_phase = jnp.sin(phase)
        stages.append(
            (
                amps[0] * cos_phase + amps[2] * sin_phase,
                amps[1] * cos_phase + amps[3] * sin_phase,
                amps[2] * cos_phase - amps[0] * sin_phase,
                amps[3] * cos_phase - amps[1] * sin_phase,
            )
        )
    first, middle, last = stages
    for part in range(4):
        combined = (
            first[part],
            0.5 * (first[part] + middle[part]),
            (first[part] + 2.0 * middle[part]) * (1.0 / 3.0),
            (first[part] + 4.0 * middle[part] + last[part]) * (1.0 / 6.0),
        )
        for step in range(4):
            source_ref[step * 4 + part] = combined[step]
    source_ref[16] = jnp.broadcast_to(column(lead_ref[...].astype(jnp.float32)), (SUBS, LANES))


def advance_kernel(
    span,
    turned_ref,
    trig_ref,
    recv_b_ref,
    recv_a_ref,
    fields_ref,
    source_ref,
    next_ref,
    out_ref,
    work_a,
    work_b,
    sem,
):
    tiles = trig_ref.shape[1]
    piece = tiles * LANES // PIECES
    lanes = lane_iota()
    site_index = lax.axis_index("sites")
    even = lax.rem(site_index, 2) == 0
    first_site = site_index * (tiles * LANES)
    lane_position = (lanes + first_site).astype(jnp.float32)
    lead = source_ref[16]
    zero = (jnp.zeros((SUBS, LANES), jnp.float32),) * 4
    targets = (work_a, work_b, work_a, out_ref)
    copy = pltpu.make_async_copy(
        out_ref.at[:, :, pl.ds(0, piece)], next_ref.at[:, :, pl.ds(0, piece)], sem
    )

    inside = {-1: site_index > 0, tiles: site_index < lax.axis_size("sites") - 1}
    halo = {}
    for tile, near_ref, far_ref in ((-1, recv_b_ref, recv_a_ref), (tiles, recv_a_ref, recv_b_ref)):
        pack = jnp.where(even, near_ref[...], far_ref[...])
        pack = jnp.where(inside[tile], pack, zero[0])
        start = LANES - REACH if tile < 0 else 0
        blocks = []
        for part in range(5):
            shift = (start - REACH * part) % LANES
            blocks.append(pltpu.roll(pack, shift, 1) if shift else pack)
        halo[tile] = (tuple(blocks[:4]), [blocks[4][place : place + 1, :] for place in range(6)])
    halo_state = {tile: halo[tile][0] for tile in halo}

    for step in range(4):
        origin_ref = turned_ref if step == 0 else targets[step - 1]
        target_ref = targets[step]
        parts = [source_ref[step * 4 + part] for part in range(4)]
        next_halo = {}

        def load(tile):
            if tile in halo:
                return halo_state[tile]
            if tile > tiles:
                return zero
            return tuple(
                origin_ref[part, :, tile * LANES : (tile + 1) * LANES] for part in range(4)
            )

        before_up = zero
        here = load(-1)
        here_up = [shift_from_left(x) for x in here]
        here_down = [shift_from_right(x) for x in here]
        for tile in range(-1, tiles + 1):
            after = load(tile + 1)
            after_up = [shift_from_left(x) for x in after]
            after_down = [shift_from_right(x) for x in after]
            if tile not in halo or step < 3:
                if tile in halo:
                    base, rows = halo[tile]
                else:
                    at = slice(tile * LANES, (tile + 1) * LANES)
                    base = tuple(turned_ref[part, :, at] for part in range(4))
                    rows = [fields_ref[place, tile : tile + 1, :] for place in range(4)]
                    rows += [trig_ref[place, tile : tile + 1, :] for place in range(2)]
                hops = [
                    jnp.where(lanes == 0, b, a) + jnp.where(lanes == LANES - 1, d, c)
                    for a, b, c, d in zip(here_up, before_up, here_down, after_down)
                ]
                masked = region_masks(
                    lane_position + float(tile * LANES), lead, span, rows[4], rows[5]
                )
                out = horner(
                    base, here, hops, rows[:4], source_terms(parts, *masked), STEP_COEF[step]
                )
                if tile in halo:
                    next_halo[tile] = tuple(jnp.where(inside[tile], x, zero[0]) for x in out)
                else:
                    if step == 3:
                        out = rotate_fore(out, rows[4], rows[5])
                    for part in range(4):
                        target_ref[part, :, at] = out[part]
                    if step == 3 and (tile + 1) * LANES == piece:
                        copy.start()
            before_up, here, here_up, here_down = here_up, after, after_up, after_down
        halo_state = next_halo

    copy.wait()


def finish_kernel(
    next_in_ref,
    out_ref,
    own_ref,
    other_ref,
    corner_ref,
    corner_other_ref,
    spin_ref,
    next_ref,
    densities_ref,
    magnet_next_ref,
    densities_out,
    magnet_out,
    sems,
):
    tiles = spin_ref.shape[1]
    piece = tiles * LANES // PIECES
    rest = pl.ds(piece, tiles * LANES - piece)
    copies = [
        pltpu.make_async_copy(out_ref.at[:, :, rest], next_ref.at[:, :, rest], sems.at[0]),
        pltpu.make_async_copy(densities_out, densities_ref, sems.at[1]),
        pltpu.make_async_copy(magnet_out, magnet_next_ref, sems.at[2]),
    ]
    copies[0].start()
    totals = []
    for place in range(5):
        rows = slice(place * tiles, (place + 1) * tiles)
        totals.append(own_ref[rows, :] + other_ref[rows, :])
    products = corner_ref[...] + corner_other_ref[...]
    corner = jnp.sum(jnp.sum(products, axis=1, keepdims=True), axis=0, keepdims=True)
    row_at = lax.broadcasted_iota(jnp.int32, (tiles, LANES), 0)
    lane_at = lax.broadcasted_iota(jnp.int32, (tiles, LANES), 1)
    totals[4] = jnp.where((row_at == tiles - 1) & (lane_at == LANES - 1), corner, totals[4])
    for place in range(5):
        for tile in range(tiles):
            densities_out[place : place + 1, tile * LANES : (tile + 1) * LANES] = totals[place][
                tile : tile + 1, :
            ]
    copies[1].start()
    field_x, field_y, field_z = (exchange_coupling * totals[1 + part] for part in range(3))
    magnet_x, magnet_y, magnet_z = (spin_ref[part] for part in range(3))
    torque = (
        magnet_y * field_z - magnet_z * field_y,
        magnet_z * field_x - magnet_x * field_z,
        magnet_x * field_y - magnet_y * field_x,
    )
    for part, magnet in enumerate((magnet_x, magnet_y, magnet_z)):
        advanced = magnet - spin_ref[3] * torque[part]
        for tile in range(tiles):
            magnet_out[part : part + 1, tile * LANES : (tile + 1) * LANES] = advanced[
                tile : tile + 1, :
            ]
    copies[2].start()
    for copy in copies:
        copy.wait()


def local(
    wave_state,
    potential,
    spin_angle,
    magnet,
    magnetic_mask,
    mode_weight,
    source_amp,
    mode_group,
    energies,
    lead_site,
):
    local_modes, local_sites = wave_state.shape[1:]
    site_count = lax.axis_size("sites")
    mode_count = lax.axis_size("modes")
    assert local_modes == SUBS and local_sites % (LANES * PIECES) == 0
    tiles = local_sites // LANES
    span = float(local_sites * site_count // 8)
    f32 = jnp.float32
    vmem = pl.BlockSpec(memory_space=pltpu.VMEM)
    anywhere = pl.BlockSpec(memory_space=pl.ANY)
    dense = (tiles, LANES)
    kept = lambda array: pltpu.with_memory_space_constraint(array, pltpu.VMEM)

    potential = potential.reshape(dense)
    spin_angle = spin_angle.reshape(dense)
    magnetic_mask = magnetic_mask.reshape(dense)

    row = lambda array: array.reshape(1, -1)
    small = (row(mode_weight), source_amp, row(mode_group), row(energies), row(lead_site))
    site_arrays = (potential, magnet, magnetic_mask)
    (pack_a, pack_b, tails_a, tails_b, weight, *staged, angle_staged) = pl.pallas_call(
        edge_kernel,
        out_shape=(
            *(pltpu.VMEM((SUBS, LANES), f32) for _ in range(5)),
            *(pltpu.VMEM(array.shape, array.dtype) for array in site_arrays + small[1:]),
            pltpu.VMEM(dense, f32),
        ),
        in_specs=[anywhere] * 10,
        out_specs=[vmem] * 13,
        scratch_shapes=[
            pltpu.VMEM((2, 4, SUBS, LANES), f32),
            pltpu.VMEM(small[0].shape, f32),
            pltpu.SemaphoreType.DMA((11,)),
        ],
        name="edges",
        cost_estimate=pl.CostEstimate(flops=100_000, bytes_accessed=200_000, transcendentals=0),
    )(wave_state, potential, spin_angle, magnet, magnetic_mask, *small)

    wave_late, pack_b = lax.optimization_barrier((wave_state, pack_b))
    turned, trig, payload = pl.pallas_call(
        functools.partial(density_kernel, local_modes * mode_count),
        out_shape=(
            pltpu.VMEM(wave_state.shape, f32),
            pltpu.VMEM((2,) + dense, f32),
            pltpu.VMEM((5 * tiles, LANES), f32),
        ),
        in_specs=[vmem] * 3,
        out_specs=[vmem] * 3,
        name="densities",
        cost_estimate=pl.CostEstimate(flops=10_000_000, bytes_accessed=1_500_000, transcendentals=0),
    )(kept(wave_late), kept(angle_staged), kept(weight))
    payload, pack_a = lax.optimization_barrier((payload, pack_a))

    def swap_sites(pack, pairs):
        partner = {i: j for pair in pairs for i, j in (pair, pair[::-1])}
        whole = [
            (
                m * site_count + s,
                m * site_count + partner[s] if s in partner else (m ^ 1) * site_count + s,
            )
            for m in range(mode_count)
            for s in range(site_count)
        ]
        return lax.ppermute(pack, ("modes", "sites"), whole)

    def swap_modes(array, distance):
        return lax.ppermute(array, "modes", [(i, i ^ distance) for i in range(mode_count)])

    recv_b = swap_sites(pack_b, [(i, i + 1) for i in range(1, site_count - 1, 2)])
    recv_a = swap_sites(pack_a, [(i, i + 1) for i in range(0, site_count - 1, 2)])
    distance = 1
    while 2 * distance < mode_count:
        payload = payload + swap_modes(payload, distance)
        distance *= 2
    last_distance = distance + 1 if distance > 1 else distance
    payload, weight = lax.optimization_barrier((payload, weight))
    payload_other = swap_modes(payload, last_distance)

    fields, source, spin, scaled = pl.pallas_call(
        functools.partial(setup_kernel, 2.0 / math.sqrt(local_modes * mode_count)),
        out_shape=(
            pltpu.VMEM((4,) + dense, f32),
            pltpu.VMEM((17, SUBS, LANES), f32),
            pltpu.VMEM((4,) + dense, f32),
            pltpu.VMEM((SUBS, LANES), f32),
        ),
        in_specs=[vmem] * 9,
        out_specs=[vmem] * 4,
        name="setup",
        cost_estimate=pl.CostEstimate(flops=1_000_000, bytes_accessed=200_000, transcendentals=0),
    )(kept(weight), kept(trig), *(kept(array) for array in staged))

    product = scaled * (tails_b * recv_b + tails_a * recv_a)
    distance = 1
    while 2 * distance < mode_count:
        product = product + swap_modes(product, distance)
        distance *= 2
    product_other = swap_modes(product, last_distance)


    next_state, advanced = pl.pallas_call(
        functools.partial(advance_kernel, span),
        out_shape=(
            jax.ShapeDtypeStruct(wave_state.shape, f32),
            pltpu.VMEM(wave_state.shape, f32),
        ),
        in_specs=[vmem] * 6,
        out_specs=[anywhere, vmem],
        scratch_shapes=[pltpu.VMEM(wave_state.shape, f32)] * 2 + [pltpu.SemaphoreType.DMA],
        name="advance",
        cost_estimate=pl.CostEstimate(flops=20_000_000, bytes_accessed=1_500_000, transcendentals=0),
    )(kept(turned), kept(trig), kept(recv_b), kept(recv_a), kept(fields), kept(source))

    return pl.pallas_call(
        finish_kernel,
        out_shape=(
            jax.ShapeDtypeStruct(wave_state.shape, f32),
            jax.ShapeDtypeStruct((5, local_sites), f32),
            jax.ShapeDtypeStruct((3, local_sites), f32),
        ),
        in_specs=[anywhere] + [vmem] * 6,
        out_specs=[anywhere] * 3,
        scratch_shapes=[
            pltpu.VMEM((5, local_sites), f32),
            pltpu.VMEM((3, local_sites), f32),
            pltpu.SemaphoreType.DMA((3,)),
        ],
        input_output_aliases={0: 0},
        name="finish",
        cost_estimate=pl.CostEstimate(flops=1_000_000, bytes_accessed=400_000, transcendentals=0),
    )(
        next_state,
        kept(advanced),
        kept(payload),
        kept(payload_other),
        kept(product),
        kept(product_other),
        kept(spin),
    )


def solution(mesh):
    return jax.shard_map(
        local,
        mesh=mesh,
        in_specs=(
            P(None, "modes", "sites"),
            P("sites"),
            P("sites"),
            P(None, "sites"),
            P("sites"),
            P("modes"),
            P(None, "modes"),
            P("modes"),
            P(),
            P("modes"),
        ),
        out_specs=(P(None, "modes", "sites"), P(None, "sites"), P(None, "sites")),
        check_vma=False,
    )
```

time: 15.7 us -> 14.1 us (0.90)
  the two profiles are of different devices: /device:TPU:9 before, /device:TPU:0 now
where the time goes in v4:
time: 14.1 us; the launch traced here: 13.9 us
  starting transfers between devices  7.34 us (52%)
  Pallas kernels  4.75 us (34%)
  waiting for transfers between devices  1.08 us (8%)
  between operations  0.71 us (5%)
    ppermute x2, starting transfers between devices, swap_sites(): return lax.ppermute(pack, ('modes', 'sites'), whole)  4.11 us
    ppermute x4, starting transfers between devices, swap_modes(): lax.ppermute(array, 'modes', [(i, i ^ distance) for i in range(mode_count)])  3.23 us
    pallas_call x1, Pallas kernels, local(): pl.pallas_call(functools.partial(advance_kernel, span), out_shape=(jax.Sh...  2.02 us
    pallas_call x1, Pallas kernels, local(): pl.pallas_call(edge_kernel, out_shape=(*(pltpu.VMEM((SUBS, LANES), f32) f...  1.23 us
    pallas_call x1, Pallas kernels, local(): pl.pallas_call(finish_kernel, out_shape=(jax.ShapeDtypeStruct(wave_state....  0.84 us
    ppermute x4, waiting for transfers between devices, swap_modes(): lax.ppermute(array, 'modes', [(i, i ^ distance) for i in range(mode_count)])  0.83 us
    pallas_call x1, Pallas kernels, local(): pl.pallas_call(functools.partial(density_kernel, local_modes * mode_count...  0.44 us
  transfers between devices with their start and end apart: 6, of which 2 were waited for; matrix products, arithmetic and copies ran while one was open for 0% of the time, Pallas kernels for 16%

profile of v4, /device:TPU:0, one launch (start us, length us, event | category | flops | bytes accessed | tf_op | source)
XLA Modules:
  0.0 13.9 jit_solution(12460345016564767311)
XLA Ops:
  0.6 0.0 copy-start
  0.6 1.2 %edges.1 = (f32[8,128]{1,0:T(8,128)S(1)}, f32[8,128]{1,0:T(8,128)S(1)}, f32[8,128]{1,0:T(8,128)S(1)}, f32[8,128]{1,0:T(8,128)S(1)}, f32[8,128]{1,0:T(8,128)S(1)}...) custom-call(f32[4,8,4096]{2,1,0:T(8,128)} %wave_ref.2, ...), custom_call_target="tpu_custom_call" | custom-call | flops 100000 | bytes 200000 | tf_op jit(solution)/shard_map/edges/pallas_call | solution.py:513
  1.9 0.0 copy-done
  1.9 0.4 %densities.1 = (f32[4,8,4096]{2,1,0:T(8,128)S(1)}, f32[2,32,128]{2,1,0:T(8,128)S(1)}, f32[160,128]{1,0:T(8,128)S(1)}) custom-call(f32[4,8,4096]{2,1,0:T(8,128)S(1)} %copy-done, f32[32,128]{1,0:T(8,128)S(1)} %get-tuple-element.33.angle_ref, f32[8,128]{1,0:T(8,128)S(1)} %get-tuple-element.42.weight_ref), custom_call_target="tpu_custom_call" | custom-call | flops 10000000 | bytes 1500000 | tf_op jit(solution)/shard_map/densities/pallas_call | solution.py:532
  2.3 0.5 %collective-permute-start.2 = (f32[160,128]{1,0:T(8,128)S(1)}, f32[160,128]{1,0:T(8,128)S(1)}, u32[]{:S(2)}, u32[]{:S(2)}) collective-permute-start(f32[160,128]{1,0:T(8,128)S(1)} %get-tuple-element.41), channel_id=1, source_target_pairs={{0,8},{8,0},{16,24},{24,16},{1,9},{9,1},{17,25},{25,17},{2,10},{10... | collective-permute-start | bytes 245768 | tf_op jit(solution)/shard_map/ppermute | solution.py:559
  2.9 0.1 collective-permute-start
  2.9 4.0 %collective-permute-start.1 = (f32[8,128]{1,0:T(8,128)S(1)}, f32[8,128]{1,0:T(8,128)S(1)}, u32[]{:S(2)}, u32[]{:S(2)}) collective-permute-start(f32[8,128]{1,0:T(8,128)S(1)} %get-tuple-element.40), channel_id=1, source_target_pairs={{0,1},{1,0},{2,3},{3,2},{4,5},{5,4},{6,7},{7,6},{8,9},{9,8},{10,11... | collective-permute-start | bytes 12296 | tf_op jit(solution)/shard_map/ppermute | solution.py:556
  7.0 0.0 collective-permute-done.2
  7.0 1.1 %collective-permute-start.3 = (f32[160,128]{1,0:T(8,128)S(1)}, f32[160,128]{1,0:T(8,128)S(1)}, u32[]{:S(2)}, u32[]{:S(2)}) collective-permute-start(f32[160,128]{1,0:T(8,128)S(1)} %add.9.own_ref), channel_id=1, source_target_pairs={{0,24},{8,16},{16,8},{24,0},{1,25},{9,17},{17,9},{25,1},{2,26},{10... | collective-permute-start | bytes 245768 | tf_op jit(solution)/shard_map/ppermute | solution.py:559
  8.1 0.2 %setup.1 = (f32[4,32,128]{2,1,0:T(8,128)S(1)}, f32[17,8,128]{2,1,0:T(8,128)S(1)}, f32[4,32,128]{2,1,0:T(8,128)S(1)}, f32[8,128]{1,0:T(8,128)S(1)}) custom-call(f32[8,128]{1,0:T(8,128)S(1)} %get-tuple-element.42.weight_ref, f32[2,32,128]{2,1,0:T(8,128)S(1)} %get-tuple-element.36.trig_ref, f32[32,128]{1,0:T(8,128)S(1)} %get-tuple-element.43.potential_ref, ...), custom_call_target="tpu_custom_call" | custom-call | flops 1000000 | bytes 200000 | tf_op jit(solution)/shard_map/setup/pallas_call | solution.py:571
  8.3 0.0 collective-permute-done.recv_b_ref
  8.3 0.3 %collective-permute-done.1.recv_a_ref = f32[8,128]{1,0:T(8,128)S(1)} collective-permute-done((f32[8,128]{1,0:T(8,128)S(1)}, f32[8,128]{1,0:T(8,128)S(1)}, u32[]{:S(2)}, u32[]{:S(2)}) %collective-permute-start.1) | collective-permute-done | bytes 4128 | tf_op jit(solution)/shard_map/ppermute | solution.py:556
  8.6 0.5 %collective-permute-start.4 = (f32[8,128]{1,0:T(8,128)S(1)}, f32[8,128]{1,0:T(8,128)S(1)}, u32[]{:S(2)}, u32[]{:S(2)}) collective-permute-start(f32[8,128]{1,0:T(8,128)S(1)} %add_multiply_fusion), channel_id=1, source_target_pairs={{0,8},{8,0},{16,24},{24,16},{1,9},{9,1},{17,25},{25,17},{2,10},{10... | collective-permute-start | bytes 12296 | tf_op jit(solution)/shard_map/ppermute | solution.py:559
  9.0 0.8 %collective-permute-done.4 = f32[8,128]{1,0:T(8,128)S(1)} collective-permute-done((f32[8,128]{1,0:T(8,128)S(1)}, f32[8,128]{1,0:T(8,128)S(1)}, u32[]{:S(2)}, u32[]{:S(2)}) %collective-permute-start.4) | collective-permute-done | bytes 4128 | tf_op jit(solution)/shard_map/ppermute | solution.py:559
  9.8 1.2 %collective-permute-start.5 = (f32[8,128]{1,0:T(8,128)S(1)}, f32[8,128]{1,0:T(8,128)S(1)}, u32[]{:S(2)}, u32[]{:S(2)}) collective-permute-start(f32[8,128]{1,0:T(8,128)S(1)} %add.11.corner_ref), channel_id=1, source_target_pairs={{0,24},{8,16},{16,8},{24,0},{1,25},{9,17},{17,9},{25,1},{2,26},{10... | collective-permute-start | bytes 12296 | tf_op jit(solution)/shard_map/ppermute | solution.py:559
  11.0 2.0 %advance.1 = (f32[4,8,4096]{2,1,0:T(8,128)}, f32[4,8,4096]{2,1,0:T(8,128)S(1)}) custom-call(f32[4,8,4096]{2,1,0:T(8,128)S(1)} %get-tuple-element.35.turned_ref, f32[2,32,128]{2,1,0:T(8,128)S(1)} %get-tuple-element.36.trig_ref, f32[8,128]{1,0:T(8,128)S(1)} %collective-permute-done.recv_b_ref, f32[8,128]{1,0:T(8,128)S(1)} %collective-permute-done.1.recv_a_ref, ...), custom_call_target="tpu_custom_call" | custom-call | flops 20000000 | bytes 1500000 | tf_op jit(solution)/shard_map/advance/pallas_call | solution.py:593
  13.1 0.0 collective-permute-done.5.corner_other_ref
  13.1 0.0 collective-permute-done.3.other_ref
  13.1 0.8 %finish.1 = (f32[4,8,4096]{2,1,0:T(8,128)}, f32[5,4096]{1,0:T(8,128)}, f32[3,4096]{1,0:T(4,128)}) custom-call(f32[4,8,4096]{2,1,0:T(8,128)} %get-tuple-element.52.next_in_ref, f32[4,8,4096]{2,1,0:T(8,128)S(1)} %get-tuple-element.53.out_ref, f32[160,128]{1,0:T(8,128)S(1)} %add.9.own_ref, ...), custom_call_target="tpu_custom_call", output_to_operand_aliasing={{0}: (0, {})} | custom-call | flops 1000000 | bytes 400000 | tf_op jit(solution)/shard_map/finish/pallas_call | solution.py:606
  (3 shorter events, 0.0 us)
Async XLA Ops:
  0.6 1.2 %copy-start = (f32[4,8,4096]{2,1,0:T(8,128)S(1)}, f32[4,8,4096]{2,1,0:T(8,128)}, u32[]{:S(2)}) copy-start(f32[4,8,4096]{2,1,0:T(8,128)} %wave_ref.2) | copy-start | bytes 1572868
  2.3 4.6 %collective-permute-start.2 = (f32[160,128]{1,0:T(8,128)S(1)}, f32[160,128]{1,0:T(8,128)S(1)}, u32[]{:S(2)}, u32[]{:S(2)}) collective-permute-start(f32[160,128]{1,0:T(8,128)S(1)} %get-tuple-element.41), channel_id=1, source_target_pairs={{0,8},{8,0},{16,24},{24,16},{1,9},{9,1},{17,25},{25,17},{2,10},{10... | collective-permute-start | bytes 245768 | tf_op jit(solution)/shard_map/ppermute | solution.py:559
  2.9 5.4 %collective-permute-start = (f32[8,128]{1,0:T(8,128)S(1)}, f32[8,128]{1,0:T(8,128)S(1)}, u32[]{:S(2)}, u32[]{:S(2)}) collective-permute-start(f32[8,128]{1,0:T(8,128)S(1)} %get-tuple-element.37), channel_id=1, source_target_pairs={{0,8},{1,2},{2,1},{3,4},{4,3},{5,6},{6,5},{7,15},{8,0},{9,10},{10,... | collective-permute-start | bytes 12296 | tf_op jit(solution)/shard_map/ppermute | solution.py:556
  2.9 5.6 %collective-permute-start.1 = (f32[8,128]{1,0:T(8,128)S(1)}, f32[8,128]{1,0:T(8,128)S(1)}, u32[]{:S(2)}, u32[]{:S(2)}) collective-permute-start(f32[8,128]{1,0:T(8,128)S(1)} %get-tuple-element.40), channel_id=1, source_target_pairs={{0,1},{1,0},{2,3},{3,2},{4,5},{5,4},{6,7},{7,6},{8,9},{9,8},{10,11... | collective-permute-start | bytes 12296 | tf_op jit(solution)/shard_map/ppermute | solution.py:556
  7.0 6.1 %collective-permute-start.3 = (f32[160,128]{1,0:T(8,128)S(1)}, f32[160,128]{1,0:T(8,128)S(1)}, u32[]{:S(2)}, u32[]{:S(2)}) collective-permute-start(f32[160,128]{1,0:T(8,128)S(1)} %add.9.own_ref), channel_id=1, source_target_pairs={{0,24},{8,16},{16,8},{24,0},{1,25},{9,17},{17,9},{25,1},{2,26},{10... | collective-permute-start | bytes 245768 | tf_op jit(solution)/shard_map/ppermute | solution.py:559
  8.6 1.3 %collective-permute-start.4 = (f32[8,128]{1,0:T(8,128)S(1)}, f32[8,128]{1,0:T(8,128)S(1)}, u32[]{:S(2)}, u32[]{:S(2)}) collective-permute-start(f32[8,128]{1,0:T(8,128)S(1)} %add_multiply_fusion), channel_id=1, source_target_pairs={{0,8},{8,0},{16,24},{24,16},{1,9},{9,1},{17,25},{25,17},{2,10},{10... | collective-permute-start | bytes 12296 | tf_op jit(solution)/shard_map/ppermute | solution.py:559
  9.8 3.2 %collective-permute-start.5 = (f32[8,128]{1,0:T(8,128)S(1)}, f32[8,128]{1,0:T(8,128)S(1)}, u32[]{:S(2)}, u32[]{:S(2)}) collective-permute-start(f32[8,128]{1,0:T(8,128)S(1)} %add.11.corner_ref), channel_id=1, source_target_pairs={{0,24},{8,16},{16,8},{24,0},{1,25},{9,17},{17,9},{25,1},{2,26},{10... | collective-permute-start | bytes 12296 | tf_op jit(solution)/shard_map/ppermute | solution.py:559

commit v5 on v4

--- a/solution.py
+++ b/solution.py
@@ -111,6 +111,7 @@
     lead_ref,
     pack_a_ref,
     pack_b_ref,
+    tails_first_ref,
     tails_a_ref,
     tails_b_ref,
     weight_out_ref,
@@ -153,6 +154,7 @@
     lanes = lane_iota()
     site_index = lax.axis_index("sites")
     even = lax.rem(site_index, 2) == 0
+    first = site_index == 0
     last = site_index == lax.axis_size("sites") - 1
     zero = jnp.zeros((SUBS, LANES), jnp.float32)
     for copy in moving[:7]:
@@ -177,8 +179,10 @@
     for part in range(4):
         end = tail[(part + 2) % 4][:, LANES - 1 : LANES]
         tails = jnp.where(lanes == REACH * part, -end if part < 2 else end, tails)
-    tails_a_ref[...] = jnp.where(jnp.logical_and(even, jnp.logical_not(last)), tails, zero)
-    tails_b_ref[...] = jnp.where(jnp.logical_or(even, last), zero, tails)
+    tails = jnp.where(last, zero, tails)
+    tails_first_ref[...] = jnp.where(first, tails, zero)
+    tails_a_ref[...] = jnp.where(jnp.logical_or(first, jnp.logical_not(even)), zero, tails)
+    tails_b_ref[...] = jnp.where(even, zero, tails)
 
     rows = sub_iota()
     packs = []
@@ -325,112 +329,161 @@
     source_ref[16] = jnp.broadcast_to(column(lead_ref[...].astype(jnp.float32)), (SUBS, LANES))
 
 
-def advance_kernel(
-    span,
-    turned_ref,
-    trig_ref,
-    recv_b_ref,
-    recv_a_ref,
-    fields_ref,
-    source_ref,
-    next_ref,
-    out_ref,
-    work_a,
-    work_b,
-    sem,
-):
-    tiles = trig_ref.shape[1]
-    piece = tiles * LANES // PIECES
-    lanes = lane_iota()
+def halo_tiles(recv_first_ref, recv_b_ref, recv_a_ref, tiles):
     site_index = lax.axis_index("sites")
     even = lax.rem(site_index, 2) == 0
-    first_site = site_index * (tiles * LANES)
-    lane_position = (lanes + first_site).astype(jnp.float32)
-    lead = source_ref[16]
-    zero = (jnp.zeros((SUBS, LANES), jnp.float32),) * 4
-    targets = (work_a, work_b, work_a, out_ref)
-    copy = pltpu.make_async_copy(
-        out_ref.at[:, :, pl.ds(0, piece)], next_ref.at[:, :, pl.ds(0, piece)], sem
-    )
-
     inside = {-1: site_index > 0, tiles: site_index < lax.axis_size("sites") - 1}
     halo = {}
     for tile, near_ref, far_ref in ((-1, recv_b_ref, recv_a_ref), (tiles, recv_a_ref, recv_b_ref)):
         pack = jnp.where(even, near_ref[...], far_ref[...])
-        pack = jnp.where(inside[tile], pack, zero[0])
+        pack = jnp.where(site_index == (1 if tile < 0 else 0), recv_first_ref[...], pack)
+        pack = jnp.where(inside[tile], pack, jnp.zeros_like(pack))
         start = LANES - REACH if tile < 0 else 0
         blocks = []
         for part in range(5):
             shift = (start - REACH * part) % LANES
             blocks.append(pltpu.roll(pack, shift, 1) if shift else pack)
         halo[tile] = (tuple(blocks[:4]), [blocks[4][place : place + 1, :] for place in range(6)])
-    halo_state = {tile: halo[tile][0] for tile in halo}
-
-    for step in range(4):
-        origin_ref = turned_ref if step == 0 else targets[step - 1]
-        target_ref = targets[step]
-        parts = [source_ref[step * 4 + part] for part in range(4)]
-        next_halo = {}
-
-        def load(tile):
+    return halo, inside
+
+
+def one_step(
+    step,
+    span,
+    turned_ref,
+    trig_ref,
+    fields_ref,
+    source_ref,
+    halo,
+    inside,
+    states,
+    after_tile=None,
+):
+    tiles = fields_ref.shape[1]
+    lanes = lane_iota()
+    first_site = lax.axis_index("sites") * (tiles * LANES)
+    lane_position = (lanes + first_site).astype(jnp.float32)
+    lead = source_ref[16]
+    zero = (jnp.zeros((SUBS, LANES), jnp.float32),) * 4
+    (origin_ref, halo_state), target_ref = states
+    parts = [source_ref[step * 4 + part] for part in range(4)]
+    next_halo = {}
+
+    def load(tile):
+        if tile in halo:
+            return halo_state[tile]
+        if tile > tiles:
+            return zero
+        return tuple(origin_ref[part, :, tile * LANES : (tile + 1) * LANES] for part in range(4))
+
+    before_up = zero
+    here = load(-1)
+    here_up = [shift_from_left(x) for x in here]
+    here_down = [shift_from_right(x) for x in here]
+    for tile in range(-1, tiles + 1):
+        after = load(tile + 1)
+        after_up = [shift_from_left(x) for x in after]
+        after_down = [shift_from_right(x) for x in after]
+        if tile not in halo or step < 3:
             if tile in halo:
-                return halo_state[tile]
-            if tile > tiles:
-                return zero
-            return tuple(
-                origin_ref[part, :, tile * LANES : (tile + 1) * LANES] for part in range(4)
-            )
-
-        before_up = zero
-        here = load(-1)
-        here_up = [shift_from_left(x) for x in here]
-        here_down = [shift_from_right(x) for x in here]
-        for tile in range(-1, tiles + 1):
-            after = load(tile + 1)
-            after_up = [shift_from_left(x) for x in after]
-            after_down = [shift_from_right(x) for x in after]
-            if tile not in halo or step < 3:
-                if tile in halo:
-                    base, rows = halo[tile]
-                else:
-                    at = slice(tile * LANES, (tile + 1) * LANES)
-                    base = tuple(turned_ref[part, :, at] for part in range(4))
-                    rows = [fields_ref[place, tile : tile + 1, :] for place in range(4)]
-                    rows += [trig_ref[place, tile : tile + 1, :] for place in range(2)]
-                hops = [
-                    jnp.where(lanes == 0, b, a) + jnp.where(lanes == LANES - 1, d, c)
-                    for a, b, c, d in zip(here_up, before_up, here_down, after_down)
-                ]
-                masked = region_masks(
-                    lane_position + float(tile * LANES), lead, span, rows[4], rows[5]
-                )
-                out = horner(
-                    base, here, hops, rows[:4], source_terms(parts, *masked), STEP_COEF[step]
-                )
-                if tile in halo:
-                    next_halo[tile] = tuple(jnp.where(inside[tile], x, zero[0]) for x in out)
-                else:
-                    if step == 3:
-                        out = rotate_fore(out, rows[4], rows[5])
-                    for part in range(4):
-                        target_ref[part, :, at] = out[part]
-                    if step == 3 and (tile + 1) * LANES == piece:
-                        copy.start()
-            before_up, here, here_up, here_down = here_up, after, after_up, after_down
-        halo_state = next_halo
-
-    copy.wait()
+                base, rows = halo[tile]
+            else:
+                at = slice(tile * LANES, (tile + 1) * LANES)
+                base = tuple(turned_ref[part, :, at] for part in range(4))
+                rows = [fields_ref[place, tile : tile + 1, :] for place in range(4)]
+                rows += [trig_ref[place, tile : tile + 1, :] for place in range(2)]
+            hops = [
+                jnp.where(lanes == 0, b, a) + jnp.where(lanes == LANES - 1, d, c)
+                for a, b, c, d in zip(here_up, before_up, here_down, after_down)
+            ]
+            masked = region_masks(lane_position + float(tile * LANES), lead, span, rows[4], rows[5])
+            out = horner(base, here, hops, rows[:4], source_terms(parts, *masked), STEP_COEF[step])
+            if tile in halo:
+                next_halo[tile] = tuple(jnp.where(inside[tile], x, zero[0]) for x in out)
+            else:
+                if step == 3:
+                    out = rotate_fore(out, rows[4], rows[5])
+                for part in range(4):
+                    target_ref[part, :, at] = out[part]
+                if after_tile is not None:
+                    after_tile(tile)
+        before_up, here, here_up, here_down = here_up, after, after_up, after_down
+    return next_halo
+
+
+def first_steps_kernel(
+    span,
+    turned_ref,
+    trig_ref,
+    recv_first_ref,
+    recv_b_ref,
+    recv_a_ref,
+    fields_ref,
+    source_ref,
+    state_ref,
+    halo_ref,
+    work_ref,
+):
+    tiles = fields_ref.shape[1]
+    halo, inside = halo_tiles(recv_first_ref, recv_b_ref, recv_a_ref, tiles)
+    common = (span, turned_ref, trig_ref, fields_ref, source_ref, halo, inside)
+    values = {tile: halo[tile][0] for tile in halo}
+    values = one_step(0, *common, ((turned_ref, values), work_ref))
+    values = one_step(1, *common, ((work_ref, values), state_ref))
+    for side, tile in enumerate((-1, tiles)):
+        for part in range(4):
+            halo_ref[side, part] = values[tile][part]
+
+
+def last_steps_kernel(
+    span,
+    turned_ref,
+    trig_ref,
+    recv_first_ref,
+    recv_b_ref,
+    recv_a_ref,
+    fields_ref,
+    source_ref,
+    state_ref,
+    halo_ref,
+    next_ref,
+    work_ref,
+    out_ref,
+    sems,
+):
+    tiles = fields_ref.shape[1]
+    piece = tiles * LANES // PIECES
+    copies = [
+        pltpu.make_async_copy(
+            out_ref.at[:, :, pl.ds(part * piece, piece)],
+            next_ref.at[:, :, pl.ds(part * piece, piece)],
+            sems.at[part],
+        )
+        for part in range(PIECES)
+    ]
+    halo, inside = halo_tiles(recv_first_ref, recv_b_ref, recv_a_ref, tiles)
+    common = (span, turned_ref, trig_ref, fields_ref, source_ref, halo, inside)
+    values = {
+        tile: tuple(halo_ref[side, part] for part in range(4))
+        for side, tile in enumerate((-1, tiles))
+    }
+    values = one_step(2, *common, ((state_ref, values), work_ref))
+
+    def after_tile(tile):
+        if (tile + 1) * LANES % piece == 0:
+            copies[tile * LANES // piece].start()
+
+    one_step(3, *common, ((work_ref, values), out_ref), after_tile)
+    for copy in copies:
+        copy.wait()
 
 
 def finish_kernel(
-    next_in_ref,
-    out_ref,
     own_ref,
     other_ref,
     corner_ref,
     corner_other_ref,
     spin_ref,
-    next_ref,
     densities_ref,
     magnet_next_ref,
     densities_out,
@@ -438,14 +491,10 @@
     sems,
 ):
     tiles = spin_ref.shape[1]
-    piece = tiles * LANES // PIECES
-    rest = pl.ds(piece, tiles * LANES - piece)
     copies = [
-        pltpu.make_async_copy(out_ref.at[:, :, rest], next_ref.at[:, :, rest], sems.at[0]),
-        pltpu.make_async_copy(densities_out, densities_ref, sems.at[1]),
-        pltpu.make_async_copy(magnet_out, magnet_next_ref, sems.at[2]),
+        pltpu.make_async_copy(densities_out, densities_ref, sems.at[0]),
+        pltpu.make_async_copy(magnet_out, magnet_next_ref, sems.at[1]),
     ]
-    copies[0].start()
     totals = []
     for place in range(5):
         rows = slice(place * tiles, (place + 1) * tiles)
@@ -460,7 +509,7 @@
             densities_out[place : place + 1, tile * LANES : (tile + 1) * LANES] = totals[place][
                 tile : tile + 1, :
             ]
-    copies[1].start()
+    copies[0].start()
     field_x, field_y, field_z = (exchange_coupling * totals[1 + part] for part in range(3))
     magnet_x, magnet_y, magnet_z = (spin_ref[part] for part in range(3))
     torque = (
@@ -474,7 +523,7 @@
             magnet_out[part : part + 1, tile * LANES : (tile + 1) * LANES] = advanced[
                 tile : tile + 1, :
             ]
-    copies[2].start()
+    copies[1].start()
     for copy in copies:
         copy.wait()
 
@@ -510,15 +559,15 @@
     row = lambda array: array.reshape(1, -1)
     small = (row(mode_weight), source_amp, row(mode_group), row(energies), row(lead_site))
     site_arrays = (potential, magnet, magnetic_mask)
-    (pack_a, pack_b, tails_a, tails_b, weight, *staged, angle_staged) = pl.pallas_call(
+    (pack_a, pack_b, tails_first, tails_a, tails_b, weight, *staged, angle_staged) = pl.pallas_call(
         edge_kernel,
         out_shape=(
-            *(pltpu.VMEM((SUBS, LANES), f32) for _ in range(5)),
+            *(pltpu.VMEM((SUBS, LANES), f32) for _ in range(6)),
             *(pltpu.VMEM(array.shape, array.dtype) for array in site_arrays + small[1:]),
             pltpu.VMEM(dense, f32),
         ),
         in_specs=[anywhere] * 10,
-        out_specs=[vmem] * 13,
+        out_specs=[vmem] * 14,
         scratch_shapes=[
             pltpu.VMEM((2, 4, SUBS, LANES), f32),
             pltpu.VMEM(small[0].shape, f32),
@@ -541,7 +590,6 @@
         name="densities",
         cost_estimate=pl.CostEstimate(flops=10_000_000, bytes_accessed=1_500_000, transcendentals=0),
     )(kept(wave_late), kept(angle_staged), kept(weight))
-    payload, pack_a = lax.optimization_barrier((payload, pack_a))
 
     def swap_sites(pack, pairs):
         partner = {i: j for pair in pairs for i, j in (pair, pair[::-1])}
@@ -559,7 +607,8 @@
         return lax.ppermute(array, "modes", [(i, i ^ distance) for i in range(mode_count)])
 
     recv_b = swap_sites(pack_b, [(i, i + 1) for i in range(1, site_count - 1, 2)])
-    recv_a = swap_sites(pack_a, [(i, i + 1) for i in range(0, site_count - 1, 2)])
+    recv_a = swap_sites(pack_a, [(i, i + 1) for i in range(2, site_count - 1, 2)])
+    recv_first = swap_sites(pack_a, [(0, 1)])
     distance = 1
     while 2 * distance < mode_count:
         payload = payload + swap_modes(payload, distance)
@@ -582,53 +631,59 @@
         cost_estimate=pl.CostEstimate(flops=1_000_000, bytes_accessed=200_000, transcendentals=0),
     )(kept(weight), kept(trig), *(kept(array) for array in staged))
 
-    product = scaled * (tails_b * recv_b + tails_a * recv_a)
+    product = scaled * (tails_first * recv_first + tails_b * recv_b + tails_a * recv_a)
     distance = 1
     while 2 * distance < mode_count:
         product = product + swap_modes(product, distance)
         distance *= 2
+    common = (turned, trig, recv_first, recv_b, recv_a, fields, source)
+    state, halo_state = pl.pallas_call(
+        functools.partial(first_steps_kernel, span),
+        out_shape=(
+            pltpu.VMEM(wave_state.shape, f32),
+            pltpu.VMEM((2, 4, SUBS, LANES), f32),
+        ),
+        in_specs=[vmem] * 7,
+        out_specs=[vmem] * 2,
+        scratch_shapes=[pltpu.VMEM(wave_state.shape, f32)],
+        name="first_steps",
+        cost_estimate=pl.CostEstimate(flops=10_000_000, bytes_accessed=700_000, transcendentals=0),
+    )(*(kept(array) for array in common))
+    product, halo_state = lax.optimization_barrier((product, halo_state))
     product_other = swap_modes(product, last_distance)
 
 
-    next_state, advanced = pl.pallas_call(
-        functools.partial(advance_kernel, span),
-        out_shape=(
-            jax.ShapeDtypeStruct(wave_state.shape, f32),
+    next_state = pl.pallas_call(
+        functools.partial(last_steps_kernel, span),
+        out_shape=jax.ShapeDtypeStruct(wave_state.shape, f32),
+        in_specs=[vmem] * (len(common) + 2),
+        out_specs=anywhere,
+        scratch_shapes=[
             pltpu.VMEM(wave_state.shape, f32),
-        ),
-        in_specs=[vmem] * 6,
-        out_specs=[anywhere, vmem],
-        scratch_shapes=[pltpu.VMEM(wave_state.shape, f32)] * 2 + [pltpu.SemaphoreType.DMA],
-        name="advance",
-        cost_estimate=pl.CostEstimate(flops=20_000_000, bytes_accessed=1_500_000, transcendentals=0),
-    )(kept(turned), kept(trig), kept(recv_b), kept(recv_a), kept(fields), kept(source))
-
-    return pl.pallas_call(
+            pltpu.VMEM(wave_state.shape, f32),
+            pltpu.SemaphoreType.DMA((PIECES,)),
+        ],
+        name="last_steps",
+        cost_estimate=pl.CostEstimate(flops=10_000_000, bytes_accessed=700_000, transcendentals=0),
+    )(*(kept(array) for array in common + (state, halo_state)))
+
+    densities, magnet_next = pl.pallas_call(
         finish_kernel,
         out_shape=(
-            jax.ShapeDtypeStruct(wave_state.shape, f32),
             jax.ShapeDtypeStruct((5, local_sites), f32),
             jax.ShapeDtypeStruct((3, local_sites), f32),
         ),
-        in_specs=[anywhere] + [vmem] * 6,
-        out_specs=[anywhere] * 3,
+        in_specs=[vmem] * 5,
+        out_specs=[anywhere] * 2,
         scratch_shapes=[
             pltpu.VMEM((5, local_sites), f32),
             pltpu.VMEM((3, local_sites), f32),
-            pltpu.SemaphoreType.DMA((3,)),
+            pltpu.SemaphoreType.DMA((2,)),
         ],
-        input_output_aliases={0: 0},
         name="finish",
         cost_estimate=pl.CostEstimate(flops=1_000_000, bytes_accessed=400_000, transcendentals=0),
-    )(
-        next_state,
-        kept(advanced),
-        kept(payload),
-        kept(payload_other),
-        kept(product),
-        kept(product_other),
-        kept(spin),
-    )
+    )(kept(payload), kept(payload_other), kept(product), kept(product_other), kept(spin))
+    return (next_state, densities, magnet_next)
 
 
 def solution(mesh):

time: 14.1 us -> 13.6 us (0.965)
  the two profiles are of different devices: /device:TPU:0 before, /device:TPU:11 now
where the time goes in v5:
time: 13.6 us; the launch traced here: 13.4 us
  starting transfers between devices  7.59 us (56%)
  Pallas kernels  4.92 us (36%)
  between operations  0.73 us (5%)
  waiting for transfers between devices  0.18 us (1%)
    ppermute x4, starting transfers between devices, swap_modes(): lax.ppermute(array, 'modes', [(i, i ^ distance) for i in range(mode_count)])  6.23 us
    pallas_call x1, Pallas kernels, local(): pl.pallas_call(functools.partial(last_steps_kernel, span), out_shape=jax....  1.47 us
    ppermute x3, starting transfers between devices, swap_sites(): return lax.ppermute(pack, ('modes', 'sites'), whole)  1.35 us
    pallas_call x1, Pallas kernels, local(): pl.pallas_call(edge_kernel, out_shape=(*(pltpu.VMEM((SUBS, LANES), f32) f...  1.23 us
    pallas_call x1, Pallas kernels, local(): pl.pallas_call(finish_kernel, out_shape=(jax.ShapeDtypeStruct((5, local_s...  0.78 us
    pallas_call x1, Pallas kernels, local(): pl.pallas_call(functools.partial(first_steps_kernel, span), out_shape=(pl...  0.76 us
    pallas_call x1, Pallas kernels, local(): pl.pallas_call(functools.partial(density_kernel, local_modes * mode_count...  0.45 us
  transfers between devices with their start and end apart: 7, of which 2 were waited for; matrix products, arithmetic and copies ran while one was open for 0% of the time, Pallas kernels for 18%

profile of v5, /device:TPU:11, one launch (start us, length us, event | category | flops | bytes accessed | tf_op | source)
XLA Modules:
  0.0 13.4 jit_solution(6567060212360446721)
XLA Ops:
  0.6 0.0 copy-start
  0.6 1.2 %edges.1 = (f32[8,128]{1,0:T(8,128)S(1)}, f32[8,128]{1,0:T(8,128)S(1)}, f32[8,128]{1,0:T(8,128)S(1)}, f32[8,128]{1,0:T(8,128)S(1)}, f32[8,128]{1,0:T(8,128)S(1)}...) custom-call(f32[4,8,4096]{2,1,0:T(8,128)} %wave_ref.2, ...), custom_call_target="tpu_custom_call" | custom-call | flops 100000 | bytes 200000 | tf_op jit(solution)/shard_map/edges/pallas_call | solution.py:562
  1.9 0.0 copy-done
  1.9 0.4 %densities.1 = (f32[4,8,4096]{2,1,0:T(8,128)S(1)}, f32[2,32,128]{2,1,0:T(8,128)S(1)}, f32[160,128]{1,0:T(8,128)S(1)}) custom-call(f32[4,8,4096]{2,1,0:T(8,128)S(1)} %copy-done, f32[32,128]{1,0:T(8,128)S(1)} %get-tuple-element.36.angle_ref, f32[8,128]{1,0:T(8,128)S(1)} %get-tuple-element.43.weight_ref), custom_call_target="tpu_custom_call" | custom-call | flops 10000000 | bytes 1500000 | tf_op jit(solution)/shard_map/densities/pallas_call | solution.py:581
  2.3 0.7 %collective-permute-start.3 = (f32[160,128]{1,0:T(8,128)S(1)}, f32[160,128]{1,0:T(8,128)S(1)}, u32[]{:S(2)}, u32[]{:S(2)}) collective-permute-start(f32[160,128]{1,0:T(8,128)S(1)} %get-tuple-element.42), channel_id=1, source_target_pairs={{0,8},{8,0},{16,24},{24,16},{1,9},{9,1},{17,25},{25,17},{2,10},{10... | collective-permute-start | bytes 245768 | tf_op jit(solution)/shard_map/ppermute | solution.py:607
  3.1 0.1 collective-permute-start
  3.2 1.3 %collective-permute-start.1 = (f32[8,128]{1,0:T(8,128)S(1)}, f32[8,128]{1,0:T(8,128)S(1)}, u32[]{:S(2)}, u32[]{:S(2)}) collective-permute-start(f32[8,128]{1,0:T(8,128)S(1)} %get-tuple-element.41), channel_id=1, source_target_pairs={{0,8},{1,2},{2,1},{3,4},{4,3},{5,6},{6,5},{7,15},{8,0},{9,10},{10,... | collective-permute-start | bytes 12296 | tf_op jit(solution)/shard_map/ppermute | solution.py:604
  4.4 0.0 collective-permute-start.2
  4.4 0.0 collective-permute-done.3
  4.5 2.4 %collective-permute-start.5 = (f32[160,128]{1,0:T(8,128)S(1)}, f32[160,128]{1,0:T(8,128)S(1)}, u32[]{:S(2)}, u32[]{:S(2)}) collective-permute-start(f32[160,128]{1,0:T(8,128)S(1)} %add.12.own_ref), channel_id=1, source_target_pairs={{0,24},{8,16},{16,8},{24,0},{1,25},{9,17},{17,9},{25,1},{2,26},{10... | collective-permute-start | bytes 245768 | tf_op jit(solution)/shard_map/ppermute | solution.py:607
  6.8 0.2 %setup.1 = (f32[4,32,128]{2,1,0:T(8,128)S(1)}, f32[17,8,128]{2,1,0:T(8,128)S(1)}, f32[4,32,128]{2,1,0:T(8,128)S(1)}, f32[8,128]{1,0:T(8,128)S(1)}) custom-call(f32[8,128]{1,0:T(8,128)S(1)} %get-tuple-element.43.weight_ref, f32[2,32,128]{2,1,0:T(8,128)S(1)} %get-tuple-element.39.trig_ref, f32[32,128]{1,0:T(8,128)S(1)} %get-tuple-element.44.potential_ref, ...), custom_call_target="tpu_custom_call" | custom-call | flops 1000000 | bytes 200000 | tf_op jit(solution)/shard_map/setup/pallas_call | solution.py:620
  7.0 0.0 collective-permute-done.recv_first_ref
  7.1 0.0 collective-permute-done.1.recv_b_ref
  7.1 0.0 collective-permute-done.2.recv_a_ref
  7.1 1.7 %collective-permute-start.4 = (f32[8,128]{1,0:T(8,128)S(1)}, f32[8,128]{1,0:T(8,128)S(1)}, u32[]{:S(2)}, u32[]{:S(2)}) collective-permute-start(f32[8,128]{1,0:T(8,128)S(1)} %add_multiply_fusion), channel_id=1, source_target_pairs={{0,8},{8,0},{16,24},{24,16},{1,9},{9,1},{17,25},{25,17},{2,10},{10... | collective-permute-start | bytes 12296 | tf_op jit(solution)/shard_map/ppermute | solution.py:607
  8.8 0.8 %first_steps.1 = (f32[4,8,4096]{2,1,0:T(8,128)S(1)}, f32[2,4,8,128]{3,2,1,0:T(8,128)S(1)}) custom-call(f32[4,8,4096]{2,1,0:T(8,128)S(1)} %get-tuple-element.38.turned_ref, f32[2,32,128]{2,1,0:T(8,128)S(1)} %get-tuple-element.39.trig_ref, f32[8,128]{1,0:T(8,128)S(1)} %collective-permute-done.recv_first_ref, f32[8,128]{1,0:T(8,128)S(1)} %collective-permute-done.1.recv_b_ref, ...), custom_call_target="tpu_custom_call" | custom-call | flops 10000000 | bytes 700000 | tf_op jit(solution)/shard_map/first_steps/pallas_call | solution.py:640
  9.5 0.1 collective-permute-done.4
  9.6 1.5 %collective-permute-start.6 = (f32[8,128]{1,0:T(8,128)S(1)}, f32[8,128]{1,0:T(8,128)S(1)}, u32[]{:S(2)}, u32[]{:S(2)}) collective-permute-start(f32[8,128]{1,0:T(8,128)S(1)} %add.15.corner_ref), channel_id=1, source_target_pairs={{0,24},{8,16},{16,8},{24,0},{1,25},{9,17},{17,9},{25,1},{2,26},{10... | collective-permute-start | bytes 12296 | tf_op jit(solution)/shard_map/ppermute | solution.py:607
  11.1 1.5 %last_steps.1 = f32[4,8,4096]{2,1,0:T(8,128)} custom-call(f32[4,8,4096]{2,1,0:T(8,128)S(1)} %get-tuple-element.38.turned_ref, f32[2,32,128]{2,1,0:T(8,128)S(1)} %get-tuple-element.39.trig_ref, f32[8,128]{1,0:T(8,128)S(1)} %collective-permute-done.recv_first_ref, f32[8,128]{1,0:T(8,128)S(1)} %collective-permute-done.1.recv_b_ref, ...), custom_call_target="tpu_custom_call" | custom-call | flops 10000000 | bytes 700000 | tf_op jit(solution)/shard_map/last_steps/pallas_call | solution.py:656
  12.5 0.1 collective-permute-done.6.corner_other_ref
  12.7 0.0 collective-permute-done.5.other_ref
  12.7 0.8 %finish.1 = (f32[5,4096]{1,0:T(8,128)}, f32[3,4096]{1,0:T(4,128)}) custom-call(f32[160,128]{1,0:T(8,128)S(1)} %add.12.own_ref, f32[160,128]{1,0:T(8,128)S(1)} %collective-permute-done.5.other_ref, f32[8,128]{1,0:T(8,128)S(1)} %add.15.corner_ref, f32[8,128]{1,0:T(8,128)S(1)} %collective-permute-done.6.corner_other_ref, ...), custom_call_target="tpu_custom_call" | custom-call | flops 1000000 | bytes 400000 | tf_op jit(solution)/shard_map/finish/pallas_call | solution.py:670
  (3 shorter events, 0.0 us)
Async XLA Ops:
  0.6 1.3 %copy-start = (f32[4,8,4096]{2,1,0:T(8,128)S(1)}, f32[4,8,4096]{2,1,0:T(8,128)}, u32[]{:S(2)}) copy-start(f32[4,8,4096]{2,1,0:T(8,128)} %wave_ref.2) | copy-start | bytes 1572868
  2.3 2.1 %collective-permute-start.3 = (f32[160,128]{1,0:T(8,128)S(1)}, f32[160,128]{1,0:T(8,128)S(1)}, u32[]{:S(2)}, u32[]{:S(2)}) collective-permute-start(f32[160,128]{1,0:T(8,128)S(1)} %get-tuple-element.42), channel_id=1, source_target_pairs={{0,8},{8,0},{16,24},{24,16},{1,9},{9,1},{17,25},{25,17},{2,10},{10... | collective-permute-start | bytes 245768 | tf_op jit(solution)/shard_map/ppermute | solution.py:607
  3.1 4.0 %collective-permute-start = (f32[8,128]{1,0:T(8,128)S(1)}, f32[8,128]{1,0:T(8,128)S(1)}, u32[]{:S(2)}, u32[]{:S(2)}) collective-permute-start(f32[8,128]{1,0:T(8,128)S(1)} %get-tuple-element.40), channel_id=1, source_target_pairs={{0,1},{1,0},{2,10},{3,11},{4,12},{5,13},{6,14},{7,15},{8,9},{9,8},... | collective-permute-start | bytes 12296 | tf_op jit(solution)/shard_map/ppermute | solution.py:604
  3.2 3.9 %collective-permute-start.1 = (f32[8,128]{1,0:T(8,128)S(1)}, f32[8,128]{1,0:T(8,128)S(1)}, u32[]{:S(2)}, u32[]{:S(2)}) collective-permute-start(f32[8,128]{1,0:T(8,128)S(1)} %get-tuple-element.41), channel_id=1, source_target_pairs={{0,8},{1,2},{2,1},{3,4},{4,3},{5,6},{6,5},{7,15},{8,0},{9,10},{10,... | collective-permute-start | bytes 12296 | tf_op jit(solution)/shard_map/ppermute | solution.py:604
  4.4 2.6 %collective-permute-start.2 = (f32[8,128]{1,0:T(8,128)S(1)}, f32[8,128]{1,0:T(8,128)S(1)}, u32[]{:S(2)}, u32[]{:S(2)}) collective-permute-start(f32[8,128]{1,0:T(8,128)S(1)} %get-tuple-element.40), channel_id=1, source_target_pairs={{0,8},{1,9},{2,3},{3,2},{4,5},{5,4},{6,7},{7,6},{8,0},{9,1},{10,11... | collective-permute-start | bytes 12296 | tf_op jit(solution)/shard_map/ppermute | solution.py:604
  4.5 8.2 %collective-permute-start.5 = (f32[160,128]{1,0:T(8,128)S(1)}, f32[160,128]{1,0:T(8,128)S(1)}, u32[]{:S(2)}, u32[]{:S(2)}) collective-permute-start(f32[160,128]{1,0:T(8,128)S(1)} %add.12.own_ref), channel_id=1, source_target_pairs={{0,24},{8,16},{16,8},{24,0},{1,25},{9,17},{17,9},{25,1},{2,26},{10... | collective-permute-start | bytes 245768 | tf_op jit(solution)/shard_map/ppermute | solution.py:607
  7.1 2.5 %collective-permute-start.4 = (f32[8,128]{1,0:T(8,128)S(1)}, f32[8,128]{1,0:T(8,128)S(1)}, u32[]{:S(2)}, u32[]{:S(2)}) collective-permute-start(f32[8,128]{1,0:T(8,128)S(1)} %add_multiply_fusion), channel_id=1, source_target_pairs={{0,8},{8,0},{16,24},{24,16},{1,9},{9,1},{17,25},{25,17},{2,10},{10... | collective-permute-start | bytes 12296 | tf_op jit(solution)/shard_map/ppermute | solution.py:607
  9.6 3.1 %collective-permute-start.6 = (f32[8,128]{1,0:T(8,128)S(1)}, f32[8,128]{1,0:T(8,128)S(1)}, u32[]{:S(2)}, u32[]{:S(2)}) collective-permute-start(f32[8,128]{1,0:T(8,128)S(1)} %add.15.corner_ref), channel_id=1, source_target_pairs={{0,24},{8,16},{16,8},{24,0},{1,25},{9,17},{17,9},{25,1},{2,26},{10... | collective-permute-start | bytes 12296 | tf_op jit(solution)/shard_map/ppermute | solution.py:607
